TPU v7x, 256 devices: a whole 4x4x8 slice. The times are simulated.
256 devices in a mesh: gx: 16 (over x_lo, z), gy: 8 (over y, core), gz: 2 (over x_hi).
Axes of the slice: x: 4 (x_hi: 2, x_lo: 2; x = x_hi * 2 + x_lo), y: 4, z: 8, core: 2. Of those that a mesh axis runs over, the one named last changes fastest.
Arguments:
- integrals: bfloat16 [1024, 8, 100, 1024], P('gx', None, 'gz', 'gy'), may hold values from -6 to 6
- amplitude: bfloat16 [100, 1024, 1024], P('gz', 'gx', 'gy'), may hold values from -0.0546875 to 0.0546875
- virtual_irrep: int32 [32], replicated, may hold values from 0 to 7, as said below
- occupied_irrep: int32 [6], replicated, may hold values from 0 to 7
Outputs:
- cycle_term: float32 [1024, 8, 1024], P('gx', None, ('gy', 'gz'))
Inputs may be any that keep to these rules, and one draw needn't show every extreme that they name: `virtual_irrep`: every one of the 8 irreps labels at least one block of virtual orbitals. `occupied_irrep`: the first 4 entries label the blocks of 25 occupied orbitals k, the next one the i block, the last one the j orbital.
All inputs are finite; a program needn't handle non-finite values.
Results may differ from a plain program's by a relative error of at most 0.0003.
Values may be sent and summed in bfloat16 or wider, within the bound.
No kernel may reach another device: no remote copies, remote signals or barrier semaphores. Data moves between devices by JAX's collectives and lax.ppermute only.
A program may use at most 64 MiB of HBM per device.

v0:
```python
import jax
import jax.numpy as jnp
from jax import lax
from jax.sharding import PartitionSpec as P

K = 100
VB = 32
KB = 25


def body(integrals, amplitude, virtual_irrep, occupied_irrep):
    rows_a, width_i, rows_k, rows_c = integrals.shape
    vlabels = jnp.repeat(virtual_irrep, VB)
    klabels = jnp.repeat(occupied_irrep[: K // KB], KB)
    irrep_left = occupied_irrep[K // KB]
    irrep_right = occupied_irrep[K // KB + 1]
    a_labels = lax.dynamic_slice_in_dim(vlabels, lax.axis_index("gx") * rows_a, rows_a)
    c_labels = lax.dynamic_slice_in_dim(vlabels, lax.axis_index("gy") * rows_c, rows_c)
    k_labels = lax.dynamic_slice_in_dim(klabels, lax.axis_index("gz") * rows_k, rows_k)
    left_key = jnp.bitwise_xor(
        jnp.bitwise_xor(a_labels[:, None, None], k_labels[None, :, None]),
        jnp.bitwise_xor(c_labels[None, None, :], irrep_left),
    )
    masked = jnp.where((left_key == 0)[:, None, :, :], integrals, jnp.zeros((), integrals.dtype))
    masked = masked.reshape(rows_a * width_i, rows_k, rows_c)
    right_key = jnp.bitwise_xor(jnp.bitwise_xor(k_labels[:, None], c_labels[None, :]), irrep_right)
    piece = lax.all_gather(amplitude, "gx", axis=1, tiled=True)
    keep_amp = jnp.bitwise_xor(right_key[:, None, :], vlabels[None, :, None]) == 0
    terms = lax.dot_general(
        masked,
        jnp.where(keep_amp, piece, jnp.zeros((), piece.dtype)),
        (((1, 2), (0, 2)), ((), ())),
        preferred_element_type=jnp.float32,
    )
    share = lax.psum_scatter(terms, ("gy", "gz"), scatter_dimension=1, tiled=True)
    return share.reshape(rows_a, width_i, share.shape[1])


def solution(mesh):
    return jax.shard_map(
        body,
        mesh=mesh,
        in_specs=(P("gx", None, "gz", "gy"), P("gz", "gx", "gy"), P(), P()),
        out_specs=P("gx", None, ("gy", "gz")),
        check_vma=False,
    )
```

profile of v0, /device:TPU:1, one launch (start us, length us, event | category | flops | bytes accessed | tf_op | source)
XLA Modules:
  0.0 259.5 jit_solution(5340903525458491368)
XLA Ops:
  6.5 0.0 all-gather.2.cloned.1.call-start
  6.5 0.7 all-gather.2.cloned.1.call-update
  7.3 0.0 reduce-scatter.2.cloned.1.call-start
  7.3 0.7 broadcast_in_dim.30
  8.0 0.1 reshape.74
  8.1 0.7 broadcast_in_dim.29
  8.8 0.1 reshape.73
  8.9 0.1 dynamic_slice.10
  9.0 0.1 dynamic_slice.9
  9.1 1.4 fusion.17
  10.5 0.7 broadcast_xor_fusion.1
  11.2 0.1 broadcast_xor_fusion
  11.2 0.7 xor_xor_fusion
  11.9 0.7 xor_compare_fusion.1
  12.6 148.8 %all-gather.2.cloned.1.call-done = bf16[50,1024,128]{2,1,0:T(8,128)(2,1)} async-done(((bf16[50,64,128]{2,1,0:T(8,128)(2,1)}), bf16[50,1024,128]{2,1,0:T(8,128)(2,1)}) %all-gather.2.cloned.1.call-update) | async-done | bytes 13107216 | tf_op jit(solution)/shard_map/all_gather | solution.py:27
  161.3 14.9 %fusion.10 = f32[512,1024]{0,1:T(8,128)} fusion(bf16[50,1024,128]{2,1,0:T(8,128)(2,1)} %all-gather.2.cloned.1.call-done, s32[1024]{0:T(1024)S(1)} %reshape.73, s32[50,128]{1,0:T(8,128)S(1)} %xor_xor_fusion, bf16[64,8,50,128]{3,1,2,0:T(8,128)(2,1)} %param.4, pred[64,50,128]{2,0,1:T(8,128)(4,1)S(1)} %xor_compare_fusion.1), kind=kOutput, calls=%fused_computation.12 | convolution fusion | flops 6733824000 | bytes 22197248 | tf_op jit(solution)/shard_map/dot_general | solution.py:29
  176.2 0.0 reduce-scatter.2.cloned.1.call-update
  176.3 74.6 %reduce-scatter.2.cloned.1.call-done = f32[512,64]{0,1:T(8,128)} async-done(((f32[512,1024]{0,1:T(8,128)}), f32[512,64]{0,1:T(8,128)}) %reduce-scatter.2.cloned.1.call-update) | async-done | bytes 131088 | tf_op jit(solution)/shard_map/reduce_scatter | solution.py:35
  250.9 1.7 copy.7
Async XLA Ops:
  6.5 154.8 %all-gather.2.cloned.1.call-start = ((), (), s32[]{:S(2)}) async-start(), calls=%async_computation.1 | async-start | bytes 13926400 | tf_op jit(solution)/shard_map/all_gather | solution.py:27
  7.3 243.6 %reduce-scatter.2.cloned.1.call-start = ((), (), s32[]{:S(2)}) async-start(), calls=%async_computation.2 | async-start | bytes 2228224 | tf_op jit(solution)/shard_map/reduce_scatter | solution.py:35
Sparse Core Ops, SparseCore 0:
  9.1 152.1 all-gather.1
  176.4 74.4 reduce-scatter.1
where the time goes:
time: 260 us; the launch traced here: 259 us
  waiting for transfers between devices  224 us (86%)
  matrix products  14.9 us (6%)
  between operations  13.4 us (5%)
  local copies, waits for them, and re-layouts  4.88 us (2%)
    all_gather x1, waiting for transfers between devices, body(): piece = lax.all_gather(amplitude, 'gx', axis=1, tiled=True)  149 us
    reduce_scatter x1, waiting for transfers between devices, body(): lax.psum_scatter(terms, ('gy', 'gz'), scatter_dimension=1, tiled=True)  74.6 us
    dot_general x1, matrix products, body(): lax.dot_general(masked, jnp.where(keep_amp, piece, jnp.zeros((), piece.dt...  14.9 us
  transfers between devices with their start and end apart: 2, of which 2 were waited for; matrix products, arithmetic and copies ran while one was open for 2% of the time, Pallas kernels for 0%

commit v1 on v0

v1 whole, which is shorter than its diff:
```python
import jax
import jax.numpy as jnp
from jax import lax
from jax.experimental import pallas as pl
from jax.experimental.pallas import tpu as pltpu
from jax.sharding import PartitionSpec as P

K = 100
VB = 32
KB = 25
HALF = 13
GROUPS = 3
SLOTS = 8
SMEM = pltpu.MemorySpace.SMEM
VMEM = pltpu.MemorySpace.VMEM
I32 = jnp.int32
F32 = jnp.float32
BF16 = jnp.bfloat16


def tier_kernel(lv, lo, out):
    rows = lax.broadcasted_iota(I32, (32, 128), 0)
    lanes = lax.broadcasted_iota(I32, (32, 128), 1)
    col = jnp.zeros((32, 128), I32)
    row = jnp.full((32, 128), 64, I32)
    for block in range(32):
        col = jnp.where(rows == block, lv[block], col)
        row = jnp.where(lanes == block, lv[block], row)
    right = lo[5]
    both = jnp.bitwise_xor(col, row)
    even = (jnp.bitwise_and(rows, 1) == 0) & (lanes < 32)
    load = jnp.zeros((), I32)
    for part in range(2):
        total = jnp.zeros((32, 128), I32)
        for kap in range(2):
            total += jnp.where(both == jnp.bitwise_xor(lo[2 * part + kap], right), 1, 0)
        for shift in (127, 126, 124):
            total = total + pltpu.roll(total, shift, 1)
        total = total + pltpu.roll(total, 31, 0)
        load = jnp.maximum(load, jnp.max(jnp.where(even & (jnp.bitwise_and(lanes, 7) == 0), total, 0)))
    most = jnp.max(jnp.sum(jnp.where(both == 0, 1, 0), axis=1))
    out[0] = jnp.where((load <= 4 * GROUPS) & (most <= SLOTS), 0, 1)


def pack_kernel(lv, lo, own, other, out):
    gx, gy, gz = lax.axis_index("gx"), lax.axis_index("gy"), lax.axis_index("gz")
    core = gy % 2
    lanes = lax.broadcasted_iota(I32, (HALF, 32, 128), 2)
    out[...] = jnp.zeros_like(out)
    room = 2 * GROUPS

    def add(amp, plane, mine):
        def step(index, carry):
            seen, unit = carry
            beta, kap, gam = index // 8, (index // 4) % 2, index % 4
            hit = lo[2 * gz + kap] ^ lv[4 * (gy - core + plane) + gam] ^ lv[2 * gx + beta] ^ lo[5] == 0
            put = hit & ((seen < room) == mine)

            @pl.when(put)
            def _():
                spot = (unit % 2) * 64
                value = out[unit // 2].astype(F32)
                for half in range(2):
                    part = amp[pl.ds(kap * KB + 12 * half, HALF), pl.ds(pl.multiple_of(beta * 32, 32), 32), :]
                    to = spot + 32 * half
                    moved = pltpu.roll(part.astype(F32), jnp.bitwise_and(to - gam * 32 + 128, 127), 2)
                    value = jnp.where((lanes >= to) & (lanes < to + 32), moved, value)
                out[unit // 2] = value.astype(BF16)

            return seen + jnp.where(hit, 1, 0), unit + jnp.where(put, 1, 0)

        return lambda unit: lax.fori_loop(0, 16, step, (jnp.zeros((), I32), unit))[1]

    unit = add(own, core, True)(jnp.zeros((), I32))
    add(other, 1 - core, False)(unit)


def main_kernel(lv, lo, w_own, w_other, *refs):
    chunks = refs[:16]
    keep, send = refs[16:18]
    w, spare, t, acc, pairs, units, blocks, busy, w_sem, spare_sem = refs[18:]
    gx, gy, gz = lax.axis_index("gx"), lax.axis_index("gy"), lax.axis_index("gz")
    core = gy % 2
    x, z = gx // 8, gx % 8
    load_w = pltpu.make_async_copy(w_own, w, w_sem)
    load_w.start()
    keep[...] = jnp.zeros_like(keep)
    send[...] = jnp.zeros_like(send)
    room = 2 * GROUPS

    shift = lo[4] ^ lo[5]
    for plane in range(2):
        for label in range(8):
            units[plane, label] = 0
    for plane in range(2):
        first_c = 4 * (gy if plane == 0 else gy + 1 - 2 * core)
        for kap in range(2):
            for gam in range(4):
                label = lo[2 * gz + kap] ^ lv[first_c + gam] ^ lo[5]
                spot = units[plane, label]
                for alpha in range(2):
                    @pl.when(label == lv[2 * gx + alpha] ^ shift)
                    def _():
                        pairs[alpha * 16 + plane * 8 + spot] = kap * 4 + gam
                units[plane, label] = spot + 1
    lanes = lax.broadcasted_iota(I32, (HALF, 32, 128), 2)

    def half_of_a(alpha, _):
        want = lv[2 * gx + alpha] ^ shift
        for block in range(4):
            busy[block] = 0

        slot = jnp.zeros((), I32)
        for p in range(16):
            source = (x ^ (p // 8)) * 8 + ((z + p) % 8)

            def arrival(beta, slot, p=p, source=source):
                block = 2 * source + beta
                hit = lv[block] == want

                @pl.when(hit)
                def _():
                    blocks[slot] = block
                    own_first = jnp.where(beta == 0, 0, units[0, lv[2 * source]])
                    far_first = jnp.where(beta == 0, 0, units[1, lv[2 * source]])
                    own_here = units[0, lv[2 * source]] + units[0, lv[2 * source + 1]]
                    near = jnp.clip(room - own_first, 0, units[0, want])
                    skip = jnp.clip(room - far_first, 0, units[1, want])
                    total = near + units[1, want] - skip

                    def place(i, _):
                        far = jnp.where(i < near, 0, 1)
                        r = jnp.where(far == 0, i, i - near + skip)
                        unit = jnp.where(far == 0, own_first + r, own_here + far_first + r - room)
                        pair = pairs[alpha * 16 + far * 8 + r]
                        line, gam = far * 2 + pair // 4, pair % 4

                        @pl.when(busy[line] == 0)
                        def _():
                            t[pl.ds(line * KB, KB)] = jnp.zeros((KB, 32 * SLOTS, 128), BF16)
                            busy[line] = 1

                        spot = (unit % 2) * 64
                        whole = chunks[p][unit // 2].astype(F32)
                        inside = (lanes >= gam * 32) & (lanes < gam * 32 + 32)
                        for half in range(2):
                            moved = pltpu.roll(whole, jnp.bitwise_and(gam * 32 - spot - 32 * half + 256, 127), 2)
                            at = (pl.ds(line * KB + 12 * half, HALF), pl.ds(pl.multiple_of(slot * 32, 32), 32), slice(None))
                            t[at] = jnp.where(inside, moved, t[at].astype(F32)).astype(BF16)
                        return 0

                    lax.fori_loop(0, total, place, 0)

                return slot + jnp.where(hit, 1, 0)

            slot = lax.fori_loop(0, 2, arrival, slot)

        @pl.when(alpha == 0)
        def _():
            load_w.wait()

        acc[...] = jnp.zeros_like(acc)

        def multiply(block, _):
            def run(source, row, first):
                lhs = [t[block * KB + k] for k in range(KB)]
                rhs = [source[pl.ds(row, 32), first + k].reshape(256, 128) for k in range(KB)]
                acc[...] += lax.dot_general(
                    jnp.concatenate(lhs, axis=1),
                    jnp.concatenate(rhs, axis=1),
                    (((1,), (1,)), ((), ())),
                    preferred_element_type=F32,
                )

            @pl.when(busy[block] == 1)
            def _():
                @pl.when(block >= 2)
                def _():
                    part = w_other.at[pl.ds(alpha * 32, 32), pl.ds((block - 2) * KB, KB)]
                    load = pltpu.make_async_copy(part, spare, spare_sem)
                    load.start()
                    load.wait()
                    run(spare, 0, 0)

                @pl.when(block < 2)
                def _():
                    run(w, alpha * 32, block * KB)

            return 0

        lax.fori_loop(0, 4, multiply, 0)

        def give(j, _):
            value = acc[pl.ds(pl.multiple_of(j * 32, 32), 32), :]

            @pl.when(alpha == core)
            def _():
                keep[blocks[j]] = value

            @pl.when(alpha != core)
            def _():
                send[blocks[j]] = value

            return 0

        lax.fori_loop(0, slot, give, 0)
        return 0

    lax.fori_loop(0, 2, half_of_a, 0)


def last_kernel(lv, lo, parts, out):
    gx, gy, gz = lax.axis_index("gx"), lax.axis_index("gy"), lax.axis_index("gz")
    dest = gy * 2 + gz
    shift = lo[4] ^ lo[5]
    for alpha in range(2):
        label = lv[2 * gx + alpha] ^ shift
        cols = []
        for beta in range(2):
            total = jnp.zeros((32, 256), F32)
            for y in range(4):
                for g in range(2):
                    total = total + parts[2 * (y * 4 + alpha * 2 + g) + beta]
            cols.append(jnp.where(lv[2 * dest + beta] == label, total, 0.0))
        out[alpha * 256 : alpha * 256 + 256, :] = jnp.concatenate(cols, axis=0).T


def gather_ring(mine):
    up = [(i, (i // 8) * 8 + (i + 1) % 8) for i in range(16)]
    down = [(i, (i // 8) * 8 + (i + 7) % 8) for i in range(16)]
    cross = [(i, (i + 8) % 16) for i in range(16)]
    zp = lambda v: lax.ppermute(v, "gx", up)
    zm = lambda v: lax.ppermute(v, "gx", down)
    xx = lambda v: lax.ppermute(v, "gx", cross)
    hold = lax.optimization_barrier
    p1, m1, o0 = hold((zp(mine), zm(mine), xx(mine)))
    p2, m2, o1 = hold((zp(p1), zm(m1), xx(m1)))
    p3, m3, o7 = hold((zp(p2), zm(m2), xx(p1)))
    p4, o2, o3 = hold((zp(p3), zm(o1), xx(m3)))
    o6, o4, o5 = hold((zp(o7), zm(o3), xx(p3)))
    return [mine, m1, m2, m3, p4, p3, p2, p1, o0, o1, o2, o3, o4, o5, o6, o7]


def sparse(tier, integrals, amplitude, virtual_irrep, occupied_irrep):
    smem = pl.BlockSpec(memory_space=SMEM)
    vmem = pl.BlockSpec(memory_space=VMEM)
    hbm = pl.BlockSpec(memory_space=pl.ANY)
    chunk = (GROUPS, HALF, 32, 128)
    params = pltpu.CompilerParams(vmem_limit_bytes=32 * 2**20)
    swap = lambda v: lax.ppermute(v, "gy", [(i, i ^ 1) for i in range(8)])
    w = jnp.transpose(integrals, (0, 2, 1, 3))
    amp_other, tier = lax.optimization_barrier((swap(amplitude), tier))
    packed = pl.pallas_call(
        pack_kernel,
        out_shape=jax.ShapeDtypeStruct(chunk, BF16),
        in_specs=[smem, smem, vmem, vmem],
        out_specs=vmem,
        compiler_params=params,
        name="pack",
    )(virtual_irrep, occupied_irrep, amplitude, amp_other)
    packed, w = lax.optimization_barrier((packed, w))
    w_other = swap(w)
    chunks = gather_ring(packed)
    keep, send = pl.pallas_call(
        main_kernel,
        out_shape=[jax.ShapeDtypeStruct((32, 32, 256), F32)] * 2,
        in_specs=[smem, smem, hbm, hbm] + [vmem] * 16,
        out_specs=[vmem, vmem],
        scratch_shapes=[
            pltpu.VMEM((64, 50, 8, 128), BF16),
            pltpu.VMEM((32, KB, 8, 128), BF16),
            pltpu.VMEM((100, 32 * SLOTS, 128), BF16),
            pltpu.VMEM((32 * SLOTS, 256), F32),
            pltpu.SMEM((32,), I32),
            pltpu.SMEM((2, 8), I32),
            pltpu.SMEM((32,), I32),
            pltpu.SMEM((4,), I32),
            pltpu.SemaphoreType.DMA,
            pltpu.SemaphoreType.DMA,
        ],
        compiler_params=params,
        name="main",
    )(virtual_irrep, occupied_irrep, w, w_other, *chunks)
    parts = lax.all_to_all(keep + swap(send), ("gy", "gz"), 0, 0, tiled=True)
    out = pl.pallas_call(
        last_kernel,
        out_shape=jax.ShapeDtypeStruct((512, 64), F32),
        in_specs=[smem, smem, vmem],
        out_specs=vmem,
        compiler_params=params,
        name="last",
    )(virtual_irrep, occupied_irrep, parts)
    return out.reshape(64, 8, 64), tier


def dense(integrals, amplitude, virtual_irrep, occupied_irrep):
    rows_a, width_i, rows_k, rows_c = integrals.shape
    vlabels = jnp.repeat(virtual_irrep, VB)
    klabels = jnp.repeat(occupied_irrep[: K // KB], KB)
    irrep_left = occupied_irrep[K // KB]
    irrep_right = occupied_irrep[K // KB + 1]
    a_labels = lax.dynamic_slice_in_dim(vlabels, lax.axis_index("gx") * rows_a, rows_a)
    c_labels = lax.dynamic_slice_in_dim(vlabels, lax.axis_index("gy") * rows_c, rows_c)
    k_labels = lax.dynamic_slice_in_dim(klabels, lax.axis_index("gz") * rows_k, rows_k)
    left_key = a_labels[:, None, None] ^ k_labels[None, :, None] ^ c_labels[None, None, :] ^ irrep_left
    masked = jnp.where((left_key == 0)[:, None, :, :], integrals, jnp.zeros((), integrals.dtype))
    masked = masked.reshape(rows_a * width_i, rows_k, rows_c)
    right_key = k_labels[:, None] ^ c_labels[None, :] ^ irrep_right
    around = gather_ring(amplitude)
    x, z = lax.axis_index("gx") // 8, lax.axis_index("gx") % 8
    piece = jnp.stack([jnp.concatenate(around[:8], axis=1), jnp.concatenate(around[8:], axis=1)])
    piece = jnp.roll(piece.reshape(2, rows_k, 8, 64, rows_c), (x, z), (0, 2))
    piece = piece.transpose(1, 0, 2, 3, 4).reshape(rows_k, 1024, rows_c)
    keep_amp = (right_key[:, None, :] ^ vlabels[None, :, None]) == 0
    terms = lax.dot_general(
        masked,
        jnp.where(keep_amp, piece, jnp.zeros((), piece.dtype)),
        (((1, 2), (0, 2)), ((), ())),
        preferred_element_type=F32,
    )
    terms = terms.reshape(rows_a * width_i, 16, 64).transpose(1, 0, 2)
    share = lax.all_to_all(terms, ("gy", "gz"), 0, 0, tiled=True).sum(0)
    return share.reshape(rows_a, width_i, 64)


def body(integrals, amplitude, virtual_irrep, occupied_irrep):
    smem = pl.BlockSpec(memory_space=SMEM)
    tier = pl.pallas_call(
        tier_kernel,
        out_shape=jax.ShapeDtypeStruct((1,), I32),
        in_specs=[smem, smem],
        out_specs=smem,
        name="tier",
    )(virtual_irrep, occupied_irrep)
    args = integrals, amplitude, virtual_irrep, occupied_irrep
    out, tier = sparse(tier, *args)
    return lax.cond(tier[0] == 1, lambda: dense(*args), lambda: out)


def solution(mesh):
    return jax.shard_map(
        body,
        mesh=mesh,
        in_specs=(P("gx", None, "gz", "gy"), P("gz", "gx", "gy"), P(), P()),
        out_specs=P("gx", None, ("gy", "gz")),
        check_vma=False,
    )
```

time: 260 us -> 97.6 us (0.38)
  waiting for transfers between devices: 224 us -> 46.6 us
  starting transfers between devices: 0.04 us -> 35.6 us
  matrix products: 14.9 us -> 0 us
  between operations: 13.4 us -> 0.76 us
  Pallas kernels: 0 us -> 11 us
  local copies, waits for them, and re-layouts: 4.88 us -> 0.72 us
    all_gather x1 -> x0, waiting for transfers between devices: 149 us -> none  [body(): piece = lax.all_gather(amplitude, 'gx', axis=1, tiled=True)]
    reduce_scatter x1 -> x0, waiting for transfers between devices: 74.6 us -> none  [body(): lax.psum_scatter(terms, ('gy', 'gz'), scatter_dimension=1, tiled=True)]
    ppermute x0 -> x18, waiting for transfers between devices: none -> 31.7 us  [the longest x5 18.7 us: gather_ring(): zp = lambda v: lax.ppermute(v, 'gx', up)]
    ppermute x0 -> x18, starting transfers between devices: none -> 28.2 us  [the longest x3 12.4 us: sparse(): swap = lambda v: lax.ppermute(v, 'gy', [(i, i ^ 1) for i in range(8)])]
    all_to_all x0 -> x1, waiting for transfers between devices: none -> 14.9 us  [sparse(): parts = lax.all_to_all(keep + swap(send), ('gy', 'gz'), 0, 0, tiled=True)]
    dot_general x1 -> x0, matrix products: 14.9 us -> none  [body(): lax.dot_general(masked, jnp.where(keep_amp, piece, jnp.zeros((), piece.dt...]
    pallas_call x0 -> x4, Pallas kernels: none -> 11 us  [the longest x1 6.24 us: sparse(): pl.pallas_call(main_kernel, out_shape=[jax.ShapeDtypeStruct((32, 32, 256)...]
    all_to_all x0 -> x1, starting transfers between devices: none -> 7.38 us  [sparse(): parts = lax.all_to_all(keep + swap(send), ('gy', 'gz'), 0, 0, tiled=True)]
  transfers between devices with their start and end apart: 2 -> 19, of which waited for: 2 -> 13; matrix products, arithmetic and copies ran while one was open for 2% -> 0% of each run, Pallas kernels for 0% -> 2%
where the time goes in v1:
time: 97.6 us; the launch traced here: 96 us
  waiting for transfers between devices  46.6 us (48%)
  starting transfers between devices  35.6 us (36%)
  Pallas kernels  11 us (11%)
  other arithmetic  1.17 us (1%)
    ppermute x5, waiting for transfers between devices, gather_ring(): zp = lambda v: lax.ppermute(v, 'gx', up)  18.7 us
    all_to_all x1, waiting for transfers between devices, sparse(): parts = lax.all_to_all(keep + swap(send), ('gy', 'gz'), 0, 0, tiled=True)  14.9 us
    ppermute x3, starting transfers between devices, sparse(): swap = lambda v: lax.ppermute(v, 'gy', [(i, i ^ 1) for i in range(8)])  12.4 us
    ppermute x5, starting transfers between devices, gather_ring(): zm = lambda v: lax.ppermute(v, 'gx', down)  9.53 us
    all_to_all x1, starting transfers between devices, sparse(): parts = lax.all_to_all(keep + swap(send), ('gy', 'gz'), 0, 0, tiled=True)  7.38 us
    pallas_call x1, Pallas kernels, sparse(): pl.pallas_call(main_kernel, out_shape=[jax.ShapeDtypeStruct((32, 32, 256)...  6.24 us
    ppermute x5, waiting for transfers between devices, gather_ring(): xx = lambda v: lax.ppermute(v, 'gx', cross)  5.8 us
    ppermute x5, waiting for transfers between devices, gather_ring(): zm = lambda v: lax.ppermute(v, 'gx', down)  4.38 us
  transfers between devices with their start and end apart: 19, of which 13 were waited for; matrix products, arithmetic and copies ran while one was open for 0% of the time, Pallas kernels for 2%

profile of v1, /device:TPU:1, one launch (start us, length us, event | category | flops | bytes accessed | tf_op | source)
XLA Modules:
  0.0 96.0 jit_solution(12545967325590600394)
XLA Ops:
  0.0 3.2 %collective-permute-start.15 = (bf16[50,64,128]{2,1,0:T(8,128)(2,1)}, bf16[50,64,128]{2,1,0:T(8,128)(2,1)S(1)}, u32[]{:S(2)}, u32[]{:S(2)}) collective-permute-start(bf16[50,64,128]{2,1,0:T(8,128)(2,1)} %own.1), channel_id=1, source_target_pairs={{0,2},{2,0},{4,6},{6,4},{8,10},{10,8},{12,14},{14,12},{1,3},{3,1},... | collective-permute-start | bytes 2457608 | tf_op jit(solution)/shard_map/ppermute | solution.py:250
  3.2 1.6 %tier.1 = s32[1]{0:T(128)} custom-call(s32[32]{0:T(128)} %lv.7, s32[6]{0:T(128)} %lo.7), custom_call_target="tpu_custom_call" | custom-call | tf_op jit(solution)/shard_map/tier/pallas_call | solution.py:328
  5.4 2.4 %pack.1.refs_0_ = bf16[3,13,32,128]{3,2,1,0:T(8,128)(2,1)S(1)} custom-call(s32[32]{0:T(128)} %lv.7, s32[6]{0:T(128)} %lo.7, bf16[50,64,128]{2,1,0:T(8,128)(2,1)} %own.1, bf16[50,64,128]{2,1,0:T(8,128)(2,1)S(1)} %collective-permute-done.15.other), custom_call_target="tpu_custom_call" | custom-call | tf_op jit(solution)/shard_map/pack/pallas_call | solution.py:253
  8.3 3.9 %collective-permute-start.18 = (bf16[3,13,32,128]{3,2,1,0:T(8,128)(2,1)S(1)}, bf16[3,13,32,128]{3,2,1,0:T(8,128)(2,1)S(1)}, u32[]{:S(2)}, u32[]{:S(2)}) collective-permute-start(bf16[3,13,32,128]{3,2,1,0:T(8,128)(2,1)S(1)} %pack.1.refs_0_), channel_id=1, source_target_pairs={{0,112},{16,0},{32,16},{48,32},{64,48},{80,64},{96,80},{112,96},{1... | collective-permute-start | bytes 958472 | tf_op jit(solution)/shard_map/ppermute | solution.py:233
  12.2 1.2 %collective-permute-start.19 = (bf16[3,13,32,128]{3,2,1,0:T(8,128)(2,1)S(1)}, bf16[3,13,32,128]{3,2,1,0:T(8,128)(2,1)S(1)}, u32[]{:S(2)}, u32[]{:S(2)}) collective-permute-start(bf16[3,13,32,128]{3,2,1,0:T(8,128)(2,1)S(1)} %pack.1.refs_0_), channel_id=1, source_target_pairs={{0,128},{16,144},{32,160},{48,176},{64,192},{80,208},{96,224},{112... | collective-permute-start | bytes 958472 | tf_op jit(solution)/shard_map/ppermute | solution.py:234
  13.3 6.3 %collective-permute-done.17.refs_7_ = bf16[3,13,32,128]{3,2,1,0:T(8,128)(2,1)S(1)} collective-permute-done((bf16[3,13,32,128]{3,2,1,0:T(8,128)(2,1)S(1)}, bf16[3,13,32,128]{3,2,1,0:T(8,128)(2,1)S(1)}, u32[]{:S(2)}, u32[]{:S(2)}) %collective-permute-start.17) | collective-permute-done | bytes 319520 | tf_op jit(solution)/shard_map/ppermute | solution.py:232
  19.7 1.0 %collective-permute-done.19.refs_8_ = bf16[3,13,32,128]{3,2,1,0:T(8,128)(2,1)S(1)} collective-permute-done((bf16[3,13,32,128]{3,2,1,0:T(8,128)(2,1)S(1)}, bf16[3,13,32,128]{3,2,1,0:T(8,128)(2,1)S(1)}, u32[]{:S(2)}, u32[]{:S(2)}) %collective-permute-start.19) | collective-permute-done | bytes 319520 | tf_op jit(solution)/shard_map/ppermute | solution.py:234
  20.7 2.7 %collective-permute-start.21 = (bf16[3,13,32,128]{3,2,1,0:T(8,128)(2,1)S(1)}, bf16[3,13,32,128]{3,2,1,0:T(8,128)(2,1)S(1)}, u32[]{:S(2)}, u32[]{:S(2)}) collective-permute-start(bf16[3,13,32,128]{3,2,1,0:T(8,128)(2,1)S(1)} %collective-permute-done.18.refs_1_), channel_id=1, source_target_pairs={{0,112},{16,0},{32,16},{48,32},{64,48},{80,64},{96,80},{112,96},{1... | collective-permute-start | bytes 958472 | tf_op jit(solution)/shard_map/ppermute | solution.py:233
  23.3 1.3 %collective-permute-start.22 = (bf16[3,13,32,128]{3,2,1,0:T(8,128)(2,1)S(1)}, bf16[3,13,32,128]{3,2,1,0:T(8,128)(2,1)S(1)}, u32[]{:S(2)}, u32[]{:S(2)}) collective-permute-start(bf16[3,13,32,128]{3,2,1,0:T(8,128)(2,1)S(1)} %collective-permute-done.18.refs_1_), channel_id=1, source_target_pairs={{0,128},{16,144},{32,160},{48,176},{64,192},{80,208},{96,224},{112... | collective-permute-start | bytes 958472 | tf_op jit(solution)/shard_map/ppermute | solution.py:234
  24.8 4.6 %collective-permute-done.20.refs_6_ = bf16[3,13,32,128]{3,2,1,0:T(8,128)(2,1)S(1)} collective-permute-done((bf16[3,13,32,128]{3,2,1,0:T(8,128)(2,1)S(1)}, bf16[3,13,32,128]{3,2,1,0:T(8,128)(2,1)S(1)}, u32[]{:S(2)}, u32[]{:S(2)}) %collective-permute-start.20) | collective-permute-done | bytes 319520 | tf_op jit(solution)/shard_map/ppermute | solution.py:232
  30.3 2.7 %collective-permute-start.24 = (bf16[3,13,32,128]{3,2,1,0:T(8,128)(2,1)S(1)}, bf16[3,13,32,128]{3,2,1,0:T(8,128)(2,1)S(1)}, u32[]{:S(2)}, u32[]{:S(2)}) collective-permute-start(bf16[3,13,32,128]{3,2,1,0:T(8,128)(2,1)S(1)} %collective-permute-done.21.refs_2_), channel_id=1, source_target_pairs={{0,112},{16,0},{32,16},{48,32},{64,48},{80,64},{96,80},{112,96},{1... | collective-permute-start | bytes 958472 | tf_op jit(solution)/shard_map/ppermute | solution.py:233
  33.3 3.9 %collective-permute-done.25.refs_15_ = bf16[3,13,32,128]{3,2,1,0:T(8,128)(2,1)S(1)} collective-permute-done((bf16[3,13,32,128]{3,2,1,0:T(8,128)(2,1)S(1)}, bf16[3,13,32,128]{3,2,1,0:T(8,128)(2,1)S(1)}, u32[]{:S(2)}, u32[]{:S(2)}) %collective-permute-start.25) | collective-permute-done | bytes 319520 | tf_op jit(solution)/shard_map/ppermute | solution.py:234
  37.8 1.2 %collective-permute-start.28 = (bf16[3,13,32,128]{3,2,1,0:T(8,128)(2,1)S(1)}, bf16[3,13,32,128]{3,2,1,0:T(8,128)(2,1)S(1)}, u32[]{:S(2)}, u32[]{:S(2)}) collective-permute-start(bf16[3,13,32,128]{3,2,1,0:T(8,128)(2,1)S(1)} %collective-permute-done.24.refs_3_), channel_id=1, source_target_pairs={{0,128},{16,144},{32,160},{48,176},{64,192},{80,208},{96,224},{112... | collective-permute-start | bytes 958472 | tf_op jit(solution)/shard_map/ppermute | solution.py:234
  39.2 1.7 %collective-permute-done.27.refs_10_ = bf16[3,13,32,128]{3,2,1,0:T(8,128)(2,1)S(1)} collective-permute-done((bf16[3,13,32,128]{3,2,1,0:T(8,128)(2,1)S(1)}, bf16[3,13,32,128]{3,2,1,0:T(8,128)(2,1)S(1)}, u32[]{:S(2)}, u32[]{:S(2)}) %collective-permute-start.27) | collective-permute-done | bytes 319520 | tf_op jit(solution)/shard_map/ppermute | solution.py:233
  40.9 1.8 %collective-permute-start.29 = (bf16[3,13,32,128]{3,2,1,0:T(8,128)(2,1)S(1)}, bf16[3,13,32,128]{3,2,1,0:T(8,128)(2,1)S(1)}, u32[]{:S(2)}, u32[]{:S(2)}) collective-permute-start(bf16[3,13,32,128]{3,2,1,0:T(8,128)(2,1)S(1)} %collective-permute-done.25.refs_15_), channel_id=1, source_target_pairs={{0,16},{16,32},{32,48},{48,64},{64,80},{80,96},{96,112},{112,0},{1... | collective-permute-start | bytes 958472 | tf_op jit(solution)/shard_map/ppermute | solution.py:232
  42.6 4.1 %collective-permute-done.26.refs_4_ = bf16[3,13,32,128]{3,2,1,0:T(8,128)(2,1)S(1)} collective-permute-done((bf16[3,13,32,128]{3,2,1,0:T(8,128)(2,1)S(1)}, bf16[3,13,32,128]{3,2,1,0:T(8,128)(2,1)S(1)}, u32[]{:S(2)}, u32[]{:S(2)}) %collective-permute-start.26) | collective-permute-done | bytes 319520 | tf_op jit(solution)/shard_map/ppermute | solution.py:232
  46.8 3.4 %collective-permute-done.29.refs_14_ = bf16[3,13,32,128]{3,2,1,0:T(8,128)(2,1)S(1)} collective-permute-done((bf16[3,13,32,128]{3,2,1,0:T(8,128)(2,1)S(1)}, bf16[3,13,32,128]{3,2,1,0:T(8,128)(2,1)S(1)}, u32[]{:S(2)}, u32[]{:S(2)}) %collective-permute-start.29) | collective-permute-done | bytes 319520 | tf_op jit(solution)/shard_map/ppermute | solution.py:232
  50.2 2.7 %collective-permute-done.30.refs_12_ = bf16[3,13,32,128]{3,2,1,0:T(8,128)(2,1)S(1)} collective-permute-done((bf16[3,13,32,128]{3,2,1,0:T(8,128)(2,1)S(1)}, bf16[3,13,32,128]{3,2,1,0:T(8,128)(2,1)S(1)}, u32[]{:S(2)}, u32[]{:S(2)}) %collective-permute-start.30) | collective-permute-done | bytes 319520 | tf_op jit(solution)/shard_map/ppermute | solution.py:233
  52.9 6.2 %main.1 = (f32[32,32,256]{2,1,0:T(8,128)S(1)}, f32[32,32,256]{2,1,0:T(8,128)S(1)}) custom-call(s32[32]{0:T(128)} %lv.7, s32[6]{0:T(128)} %lo.7, bf16[64,50,8,128]{3,2,1,0:T(8,128)(2,1)} %bitcast.38, bf16[64,50,8,128]{3,2,1,0:T(8,128)(2,1)S(1)} %collective-permute-done.16.w_other, bf16[3,13,32,128]{3,2,1,0:T(8,128)(2,1)S(1)} %pack.1.refs_0_, ...), custom_call_target="tpu_custom_call" | custom-call | tf_op jit(solution)/shard_map/main/pallas_call | solution.py:264
  59.2 8.7 %collective-permute-start.32 = (f32[32,32,256]{2,1,0:T(8,128)S(1)}, f32[32,32,256]{2,1,0:T(8,128)S(1)}, u32[]{:S(2)}, u32[]{:S(2)}) collective-permute-start(f32[32,32,256]{2,1,0:T(8,128)S(1)} %get-tuple-element.79), channel_id=1, source_target_pairs={{0,2},{2,0},{4,6},{6,4},{8,10},{10,8},{12,14},{14,12},{1,3},{3,1},... | collective-permute-start | bytes 3145736 | tf_op jit(solution)/shard_map/ppermute | solution.py:250
  67.9 2.3 %collective-permute-done.32 = f32[32,32,256]{2,1,0:T(8,128)S(1)} collective-permute-done((f32[32,32,256]{2,1,0:T(8,128)S(1)}, f32[32,32,256]{2,1,0:T(8,128)S(1)}, u32[]{:S(2)}, u32[]{:S(2)}) %collective-permute-start.32) | collective-permute-done | bytes 1048608 | tf_op jit(solution)/shard_map/ppermute | solution.py:250
  70.2 1.2 %add.36 = f32[32,32,256]{2,1,0:T(8,128)} add(f32[32,32,256]{2,1,0:T(8,128)S(1)} %get-tuple-element.78, f32[32,32,256]{2,1,0:T(8,128)S(1)} %collective-permute-done.32) | non-fusion elementwise | flops 262144 | bytes 3145728 | tf_op jit(solution)/shard_map/add | solution.py:284
  71.4 7.4 %all-to-all-start.1 = ((f32[32,32,256]{2,1,0:T(8,128)}), f32[32,32,256]{2,1,0:T(8,128)S(1)}, u32[]{:S(2)}, u32[]{:S(2)}) async-start(f32[32,32,256]{2,1,0:T(8,128)} %add.36), calls=%async_computation.1 | async-start | bytes 2097152 | tf_op jit(solution)/shard_map/all_to_all | solution.py:284
  79.4 14.9 %all-to-all-done.1.parts = f32[32,32,256]{2,1,0:T(8,128)S(1)} async-done(((f32[32,32,256]{2,1,0:T(8,128)}), f32[32,32,256]{2,1,0:T(8,128)S(1)}, u32[]{:S(2)}, u32[]{:S(2)}) %all-to-all-start.1) | async-done | bytes 1048608 | tf_op jit(solution)/shard_map/all_to_all | solution.py:284
  (28 shorter events, 4.8 us)
Async XLA Ops:
  0.0 5.4 %collective-permute-start.15 = (bf16[50,64,128]{2,1,0:T(8,128)(2,1)}, bf16[50,64,128]{2,1,0:T(8,128)(2,1)S(1)}, u32[]{:S(2)}, u32[]{:S(2)}) collective-permute-start(bf16[50,64,128]{2,1,0:T(8,128)(2,1)} %own.1), channel_id=1, source_target_pairs={{0,2},{2,0},{4,6},{6,4},{8,10},{10,8},{12,14},{14,12},{1,3},{3,1},... | collective-permute-start | bytes 2457608 | tf_op jit(solution)/shard_map/ppermute | solution.py:250
  7.8 86.5 %copy-start.7 = (s32[6]{0:T(128)S(1)}, s32[6]{0:T(128)}, u32[]{:S(2)}) copy-start(s32[6]{0:T(128)} %lo.7) | copy-start | bytes 76
  7.8 86.5 %copy-start.8 = (s32[32]{0:T(128)S(1)}, s32[32]{0:T(128)}, u32[]{:S(2)}) copy-start(s32[32]{0:T(128)} %lv.7) | copy-start | bytes 388
  7.8 45.1 %collective-permute-start.16 = (bf16[64,50,8,128]{3,2,1,0:T(8,128)(2,1)}, bf16[64,50,8,128]{3,2,1,0:T(8,128)(2,1)S(1)}, u32[]{:S(2)}, u32[]{:S(2)}) collective-permute-start(bf16[64,50,8,128]{3,2,1,0:T(8,128)(2,1)} %bitcast.37), channel_id=1, source_target_pairs={{0,2},{2,0},{4,6},{6,4},{8,10},{10,8},{12,14},{14,12},{1,3},{3,1},... | collective-permute-start | bytes 19660808 | tf_op jit(solution)/shard_map/ppermute | solution.py:250
  8.3 11.4 %collective-permute-start.17 = (bf16[3,13,32,128]{3,2,1,0:T(8,128)(2,1)S(1)}, bf16[3,13,32,128]{3,2,1,0:T(8,128)(2,1)S(1)}, u32[]{:S(2)}, u32[]{:S(2)}) collective-permute-start(bf16[3,13,32,128]{3,2,1,0:T(8,128)(2,1)S(1)} %pack.1.refs_0_), channel_id=1, source_target_pairs={{0,16},{16,32},{32,48},{48,64},{64,80},{80,96},{96,112},{112,0},{1... | collective-permute-start | bytes 958472 | tf_op jit(solution)/shard_map/ppermute | solution.py:232
  8.3 11.4 %collective-permute-start.18 = (bf16[3,13,32,128]{3,2,1,0:T(8,128)(2,1)S(1)}, bf16[3,13,32,128]{3,2,1,0:T(8,128)(2,1)S(1)}, u32[]{:S(2)}, u32[]{:S(2)}) collective-permute-start(bf16[3,13,32,128]{3,2,1,0:T(8,128)(2,1)S(1)} %pack.1.refs_0_), channel_id=1, source_target_pairs={{0,112},{16,0},{32,16},{48,32},{64,48},{80,64},{96,80},{112,96},{1... | collective-permute-start | bytes 958472 | tf_op jit(solution)/shard_map/ppermute | solution.py:233
  12.2 8.5 %collective-permute-start.19 = (bf16[3,13,32,128]{3,2,1,0:T(8,128)(2,1)S(1)}, bf16[3,13,32,128]{3,2,1,0:T(8,128)(2,1)S(1)}, u32[]{:S(2)}, u32[]{:S(2)}) collective-permute-start(bf16[3,13,32,128]{3,2,1,0:T(8,128)(2,1)S(1)} %pack.1.refs_0_), channel_id=1, source_target_pairs={{0,128},{16,144},{32,160},{48,176},{64,192},{80,208},{96,224},{112... | collective-permute-start | bytes 958472 | tf_op jit(solution)/shard_map/ppermute | solution.py:234
  20.7 8.8 %collective-permute-start.20 = (bf16[3,13,32,128]{3,2,1,0:T(8,128)(2,1)S(1)}, bf16[3,13,32,128]{3,2,1,0:T(8,128)(2,1)S(1)}, u32[]{:S(2)}, u32[]{:S(2)}) collective-permute-start(bf16[3,13,32,128]{3,2,1,0:T(8,128)(2,1)S(1)} %collective-permute-done.17.refs_7_), channel_id=1, source_target_pairs={{0,16},{16,32},{32,48},{48,64},{64,80},{80,96},{96,112},{112,0},{1... | collective-permute-start | bytes 958472 | tf_op jit(solution)/shard_map/ppermute | solution.py:232
  20.7 8.8 %collective-permute-start.21 = (bf16[3,13,32,128]{3,2,1,0:T(8,128)(2,1)S(1)}, bf16[3,13,32,128]{3,2,1,0:T(8,128)(2,1)S(1)}, u32[]{:S(2)}, u32[]{:S(2)}) collective-permute-start(bf16[3,13,32,128]{3,2,1,0:T(8,128)(2,1)S(1)} %collective-permute-done.18.refs_1_), channel_id=1, source_target_pairs={{0,112},{16,0},{32,16},{48,32},{64,48},{80,64},{96,80},{112,96},{1... | collective-permute-start | bytes 958472 | tf_op jit(solution)/shard_map/ppermute | solution.py:233
  23.3 7.0 %collective-permute-start.22 = (bf16[3,13,32,128]{3,2,1,0:T(8,128)(2,1)S(1)}, bf16[3,13,32,128]{3,2,1,0:T(8,128)(2,1)S(1)}, u32[]{:S(2)}, u32[]{:S(2)}) collective-permute-start(bf16[3,13,32,128]{3,2,1,0:T(8,128)(2,1)S(1)} %collective-permute-done.18.refs_1_), channel_id=1, source_target_pairs={{0,128},{16,144},{32,160},{48,176},{64,192},{80,208},{96,224},{112... | collective-permute-start | bytes 958472 | tf_op jit(solution)/shard_map/ppermute | solution.py:234
  24.7 12.5 %collective-permute-start.25 = (bf16[3,13,32,128]{3,2,1,0:T(8,128)(2,1)S(1)}, bf16[3,13,32,128]{3,2,1,0:T(8,128)(2,1)S(1)}, u32[]{:S(2)}, u32[]{:S(2)}) collective-permute-start(bf16[3,13,32,128]{3,2,1,0:T(8,128)(2,1)S(1)} %collective-permute-done.17.refs_7_), channel_id=1, source_target_pairs={{0,128},{16,144},{32,160},{48,176},{64,192},{80,208},{96,224},{112... | collective-permute-start | bytes 958472 | tf_op jit(solution)/shard_map/ppermute | solution.py:234
  30.3 7.0 %collective-permute-start.23 = (bf16[3,13,32,128]{3,2,1,0:T(8,128)(2,1)S(1)}, bf16[3,13,32,128]{3,2,1,0:T(8,128)(2,1)S(1)}, u32[]{:S(2)}, u32[]{:S(2)}) collective-permute-start(bf16[3,13,32,128]{3,2,1,0:T(8,128)(2,1)S(1)} %collective-permute-done.20.refs_6_), channel_id=1, source_target_pairs={{0,16},{16,32},{32,48},{48,64},{64,80},{80,96},{96,112},{112,0},{1... | collective-permute-start | bytes 958472 | tf_op jit(solution)/shard_map/ppermute | solution.py:232
  30.3 7.0 %collective-permute-start.24 = (bf16[3,13,32,128]{3,2,1,0:T(8,128)(2,1)S(1)}, bf16[3,13,32,128]{3,2,1,0:T(8,128)(2,1)S(1)}, u32[]{:S(2)}, u32[]{:S(2)}) collective-permute-start(bf16[3,13,32,128]{3,2,1,0:T(8,128)(2,1)S(1)} %collective-permute-done.21.refs_2_), channel_id=1, source_target_pairs={{0,112},{16,0},{32,16},{48,32},{64,48},{80,64},{96,80},{112,96},{1... | collective-permute-start | bytes 958472 | tf_op jit(solution)/shard_map/ppermute | solution.py:233
  33.0 7.9 %collective-permute-start.27 = (bf16[3,13,32,128]{3,2,1,0:T(8,128)(2,1)S(1)}, bf16[3,13,32,128]{3,2,1,0:T(8,128)(2,1)S(1)}, u32[]{:S(2)}, u32[]{:S(2)}) collective-permute-start(bf16[3,13,32,128]{3,2,1,0:T(8,128)(2,1)S(1)} %collective-permute-done.22.refs_9_), channel_id=1, source_target_pairs={{0,112},{16,0},{32,16},{48,32},{64,48},{80,64},{96,80},{112,96},{1... | collective-permute-start | bytes 958472 | tf_op jit(solution)/shard_map/ppermute | solution.py:233
  37.4 9.4 %collective-permute-start.26 = (bf16[3,13,32,128]{3,2,1,0:T(8,128)(2,1)S(1)}, bf16[3,13,32,128]{3,2,1,0:T(8,128)(2,1)S(1)}, u32[]{:S(2)}, u32[]{:S(2)}) collective-permute-start(bf16[3,13,32,128]{3,2,1,0:T(8,128)(2,1)S(1)} %collective-permute-done.23.refs_5_), channel_id=1, source_target_pairs={{0,16},{16,32},{32,48},{48,64},{64,80},{80,96},{96,112},{112,0},{1... | collective-permute-start | bytes 958472 | tf_op jit(solution)/shard_map/ppermute | solution.py:232
  37.8 9.0 %collective-permute-start.28 = (bf16[3,13,32,128]{3,2,1,0:T(8,128)(2,1)S(1)}, bf16[3,13,32,128]{3,2,1,0:T(8,128)(2,1)S(1)}, u32[]{:S(2)}, u32[]{:S(2)}) collective-permute-start(bf16[3,13,32,128]{3,2,1,0:T(8,128)(2,1)S(1)} %collective-permute-done.24.refs_3_), channel_id=1, source_target_pairs={{0,128},{16,144},{32,160},{48,176},{64,192},{80,208},{96,224},{112... | collective-permute-start | bytes 958472 | tf_op jit(solution)/shard_map/ppermute | solution.py:234
  39.0 11.2 %collective-permute-start.31 = (bf16[3,13,32,128]{3,2,1,0:T(8,128)(2,1)S(1)}, bf16[3,13,32,128]{3,2,1,0:T(8,128)(2,1)S(1)}, u32[]{:S(2)}, u32[]{:S(2)}) collective-permute-start(bf16[3,13,32,128]{3,2,1,0:T(8,128)(2,1)S(1)} %collective-permute-done.23.refs_5_), channel_id=1, source_target_pairs={{0,128},{16,144},{32,160},{48,176},{64,192},{80,208},{96,224},{112... | collective-permute-start | bytes 958472 | tf_op jit(solution)/shard_map/ppermute | solution.py:234
  40.9 9.3 %collective-permute-start.29 = (bf16[3,13,32,128]{3,2,1,0:T(8,128)(2,1)S(1)}, bf16[3,13,32,128]{3,2,1,0:T(8,128)(2,1)S(1)}, u32[]{:S(2)}, u32[]{:S(2)}) collective-permute-start(bf16[3,13,32,128]{3,2,1,0:T(8,128)(2,1)S(1)} %collective-permute-done.25.refs_15_), channel_id=1, source_target_pairs={{0,16},{16,32},{32,48},{48,64},{64,80},{80,96},{96,112},{112,0},{1... | collective-permute-start | bytes 958472 | tf_op jit(solution)/shard_map/ppermute | solution.py:232
  46.8 6.1 %collective-permute-start.30 = (bf16[3,13,32,128]{3,2,1,0:T(8,128)(2,1)S(1)}, bf16[3,13,32,128]{3,2,1,0:T(8,128)(2,1)S(1)}, u32[]{:S(2)}, u32[]{:S(2)}) collective-permute-start(bf16[3,13,32,128]{3,2,1,0:T(8,128)(2,1)S(1)} %collective-permute-done.28.refs_11_), channel_id=1, source_target_pairs={{0,112},{16,0},{32,16},{48,32},{64,48},{80,64},{96,80},{112,96},{1... | collective-permute-start | bytes 958472 | tf_op jit(solution)/shard_map/ppermute | solution.py:233
  59.2 35.9 %copy-start.1 = (bf16[50,64,128]{2,1,0:T(8,128)(2,1)S(1)}, bf16[50,64,128]{2,1,0:T(8,128)(2,1)}, u32[]{:S(2)}) copy-start(bf16[50,64,128]{2,1,0:T(8,128)(2,1)} %own.1) | copy-start | bytes 2457604
  59.2 11.0 %collective-permute-start.32 = (f32[32,32,256]{2,1,0:T(8,128)S(1)}, f32[32,32,256]{2,1,0:T(8,128)S(1)}, u32[]{:S(2)}, u32[]{:S(2)}) collective-permute-start(f32[32,32,256]{2,1,0:T(8,128)S(1)} %get-tuple-element.79), channel_id=1, source_target_pairs={{0,2},{2,0},{4,6},{6,4},{8,10},{10,8},{12,14},{14,12},{1,3},{3,1},... | collective-permute-start | bytes 3145736 | tf_op jit(solution)/shard_map/ppermute | solution.py:250
  71.4 22.9 %all-to-all-start.1 = ((f32[32,32,256]{2,1,0:T(8,128)}), f32[32,32,256]{2,1,0:T(8,128)S(1)}, u32[]{:S(2)}, u32[]{:S(2)}) async-start(f32[32,32,256]{2,1,0:T(8,128)} %add.36), calls=%async_computation.1 | async-start | bytes 2097152 | tf_op jit(solution)/shard_map/all_to_all | solution.py:284
  95.3 0.7 copy-start.6

commit v2 on v1

--- a/solution.py
+++ b/solution.py
@@ -38,8 +38,7 @@
             total = total + pltpu.roll(total, shift, 1)
         total = total + pltpu.roll(total, 31, 0)
         load = jnp.maximum(load, jnp.max(jnp.where(even & (jnp.bitwise_and(lanes, 7) == 0), total, 0)))
-    most = jnp.max(jnp.sum(jnp.where(both == 0, 1, 0), axis=1))
-    out[0] = jnp.where((load <= 4 * GROUPS) & (most <= SLOTS), 0, 1)
+    out[0] = jnp.where(load <= 4 * GROUPS, 0, 1)
 
 
 def pack_kernel(lv, lo, own, other, out):
@@ -54,7 +53,7 @@
             seen, unit = carry
             beta, kap, gam = index // 8, (index // 4) % 2, index % 4
             hit = lo[2 * gz + kap] ^ lv[4 * (gy - core + plane) + gam] ^ lv[2 * gx + beta] ^ lo[5] == 0
-            put = hit & ((seen < room) == mine)
+            put = hit & ((seen < room) == mine) & (unit < room)
 
             @pl.when(put)
             def _():
@@ -105,12 +104,19 @@
                 units[plane, label] = spot + 1
     lanes = lax.broadcasted_iota(I32, (HALF, 32, 128), 2)
 
-    def half_of_a(alpha, _):
+    def count_both(i, most):
+        return tuple(n + jnp.where(lv[i] == lv[2 * gx + a] ^ shift, 1, 0) for a, n in enumerate(most))
+
+    most = lax.fori_loop(0, 32, count_both, (jnp.zeros((), I32), jnp.zeros((), I32)))
+    windows = (jnp.maximum(most[0], most[1]) + SLOTS - 1) // SLOTS
+
+    def half_of_a(index, _):
+        alpha, window = index // windows, index % windows
         want = lv[2 * gx + alpha] ^ shift
         for block in range(4):
             busy[block] = 0
 
-        slot = jnp.zeros((), I32)
+        slot = -SLOTS * window
         for p in range(16):
             source = (x ^ (p // 8)) * 8 + ((z + p) % 8)
 
@@ -118,7 +124,7 @@
                 block = 2 * source + beta
                 hit = lv[block] == want
 
-                @pl.when(hit)
+                @pl.when(hit & (slot >= 0) & (slot < SLOTS))
                 def _():
                     blocks[slot] = block
                     own_first = jnp.where(beta == 0, 0, units[0, lv[2 * source]])
@@ -131,7 +137,7 @@
                     def place(i, _):
                         far = jnp.where(i < near, 0, 1)
                         r = jnp.where(far == 0, i, i - near + skip)
-                        unit = jnp.where(far == 0, own_first + r, own_here + far_first + r - room)
+                        unit = jnp.minimum(jnp.where(far == 0, own_first + r, own_here + far_first + r - room), room - 1)
                         pair = pairs[alpha * 16 + far * 8 + r]
                         line, gam = far * 2 + pair // 4, pair % 4
 
@@ -155,7 +161,7 @@
 
             slot = lax.fori_loop(0, 2, arrival, slot)
 
-        @pl.when(alpha == 0)
+        @pl.when(index == 0)
         def _():
             load_w.wait()
 
@@ -203,13 +209,13 @@
 
             return 0
 
-        lax.fori_loop(0, slot, give, 0)
+        lax.fori_loop(0, jnp.minimum(slot, SLOTS), give, 0)
         return 0
 
-    lax.fori_loop(0, 2, half_of_a, 0)
-
-
-def last_kernel(lv, lo, parts, out):
+    lax.fori_loop(0, 2 * windows, half_of_a, 0)
+
+
+def last_kernel(lv, lo, tier, parts, other, out):
     gx, gy, gz = lax.axis_index("gx"), lax.axis_index("gy"), lax.axis_index("gz")
     dest = gy * 2 + gz
     shift = lo[4] ^ lo[5]
@@ -222,7 +228,8 @@
                 for g in range(2):
                     total = total + parts[2 * (y * 4 + alpha * 2 + g) + beta]
             cols.append(jnp.where(lv[2 * dest + beta] == label, total, 0.0))
-        out[alpha * 256 : alpha * 256 + 256, :] = jnp.concatenate(cols, axis=0).T
+        rows = slice(alpha * 256, alpha * 256 + 256)
+        out[rows, :] = jnp.where(tier[0] == 0, jnp.concatenate(cols, axis=0).T, other[rows, :])
 
 
 def gather_ring(mine):
@@ -260,6 +267,7 @@
     )(virtual_irrep, occupied_irrep, amplitude, amp_other)
     packed, w = lax.optimization_barrier((packed, w))
     w_other = swap(w)
+    args = integrals, amplitude, virtual_irrep, occupied_irrep
     chunks = gather_ring(packed)
     keep, send = pl.pallas_call(
         main_kernel,
@@ -282,15 +290,17 @@
         name="main",
     )(virtual_irrep, occupied_irrep, w, w_other, *chunks)
     parts = lax.all_to_all(keep + swap(send), ("gy", "gz"), 0, 0, tiled=True)
+    parts, late = lax.optimization_barrier((parts, tier))
+    other = lax.cond(late[0] == 1, lambda: dense(*args), lambda: jnp.zeros((512, 64), F32))
     out = pl.pallas_call(
         last_kernel,
         out_shape=jax.ShapeDtypeStruct((512, 64), F32),
-        in_specs=[smem, smem, vmem],
+        in_specs=[smem, smem, smem, vmem, vmem],
         out_specs=vmem,
         compiler_params=params,
         name="last",
-    )(virtual_irrep, occupied_irrep, parts)
-    return out.reshape(64, 8, 64), tier
+    )(virtual_irrep, occupied_irrep, tier, parts, other)
+    return out.reshape(64, 8, 64)
 
 
 def dense(integrals, amplitude, virtual_irrep, occupied_irrep):
@@ -320,7 +330,7 @@
     )
     terms = terms.reshape(rows_a * width_i, 16, 64).transpose(1, 0, 2)
     share = lax.all_to_all(terms, ("gy", "gz"), 0, 0, tiled=True).sum(0)
-    return share.reshape(rows_a, width_i, 64)
+    return share
 
 
 def body(integrals, amplitude, virtual_irrep, occupied_irrep):
@@ -333,8 +343,7 @@
         name="tier",
     )(virtual_irrep, occupied_irrep)
     args = integrals, amplitude, virtual_irrep, occupied_irrep
-    out, tier = sparse(tier, *args)
-    return lax.cond(tier[0] == 1, lambda: dense(*args), lambda: out)
+    return sparse(tier, *args)
 
 
 def solution(mesh):

time: 97.6 us -> 98.8 us (1.012); the launches traced: 96 us -> 99.1 us
  Pallas kernels: 11 us -> 15.1 us
    ppermute x3, starting transfers between devices: 12.4 us -> 8.86 us  [sparse(): swap = lambda v: lax.ppermute(v, 'gy', [(i, i ^ 1) for i in range(8)])]
    pallas_call x1, Pallas kernels: 6.24 us -> 9.13 us  [sparse(): pl.pallas_call(main_kernel, out_shape=[jax.ShapeDtypeStruct((32, 32, 256)...]
    all_to_all x1, starting transfers between devices: 7.38 us -> 10 us  [sparse(): parts = lax.all_to_all(keep + swap(send), ('gy', 'gz'), 0, 0, tiled=True)]
    pallas_call x1, Pallas kernels: 0.68 us -> 2.03 us  [sparse(): pl.pallas_call(last_kernel, out_shape=jax.ShapeDtypeStruct((512, 64), F32...]
where the time goes in v2:
time: 98.8 us; the launch traced here: 99.1 us
  waiting for transfers between devices  46.7 us (47%)
  starting transfers between devices  35.1 us (36%)
  Pallas kernels  15.1 us (15%)
  other arithmetic  1.18 us (1%)
    ppermute x5, waiting for transfers between devices, gather_ring(): zp = lambda v: lax.ppermute(v, 'gx', up)  18.4 us
    all_to_all x1, waiting for transfers between devices, sparse(): parts = lax.all_to_all(keep + swap(send), ('gy', 'gz'), 0, 0, tiled=True)  15.6 us
    all_to_all x1, starting transfers between devices, sparse(): parts = lax.all_to_all(keep + swap(send), ('gy', 'gz'), 0, 0, tiled=True)  10 us
    ppermute x5, starting transfers between devices, gather_ring(): zm = lambda v: lax.ppermute(v, 'gx', down)  9.4 us
    pallas_call x1, Pallas kernels, sparse(): pl.pallas_call(main_kernel, out_shape=[jax.ShapeDtypeStruct((32, 32, 256)...  9.13 us
    ppermute x3, starting transfers between devices, sparse(): swap = lambda v: lax.ppermute(v, 'gy', [(i, i ^ 1) for i in range(8)])  8.86 us
    ppermute x5, waiting for transfers between devices, gather_ring(): xx = lambda v: lax.ppermute(v, 'gx', cross)  5.73 us
    ppermute x5, starting transfers between devices, gather_ring(): xx = lambda v: lax.ppermute(v, 'gx', cross)  4.14 us
  transfers between devices with their start and end apart: 19, of which 13 were waited for; matrix products, arithmetic and copies ran while one was open for 0% of the time, Pallas kernels for 2%

profile of v2, /device:TPU:1, one launch (start us, length us, event | category | flops | bytes accessed | tf_op | source)
XLA Modules:
  0.0 99.1 jit_solution(13818405662843536370)
XLA Ops:
  0.0 3.2 %collective-permute-start.15 = (bf16[50,64,128]{2,1,0:T(8,128)(2,1)}, bf16[50,64,128]{2,1,0:T(8,128)(2,1)S(1)}, u32[]{:S(2)}, u32[]{:S(2)}) collective-permute-start(bf16[50,64,128]{2,1,0:T(8,128)(2,1)} %own.1), channel_id=1, source_target_pairs={{0,2},{2,0},{4,6},{6,4},{8,10},{10,8},{12,14},{14,12},{1,3},{3,1},... | collective-permute-start | bytes 2457608 | tf_op jit(solution)/shard_map/ppermute | solution.py:257
  3.2 1.6 %tier.1 = s32[1]{0:T(128)} custom-call(s32[32]{0:T(128)} %lv.7, s32[6]{0:T(128)} %lo.7), custom_call_target="tpu_custom_call" | custom-call | tf_op jit(solution)/shard_map/tier/pallas_call | solution.py:338
  5.4 2.3 %pack.1.refs_0_ = bf16[3,13,32,128]{3,2,1,0:T(8,128)(2,1)S(1)} custom-call(s32[32]{0:T(128)} %lv.7, s32[6]{0:T(128)} %lo.7, bf16[50,64,128]{2,1,0:T(8,128)(2,1)} %own.1, bf16[50,64,128]{2,1,0:T(8,128)(2,1)S(1)} %collective-permute-done.15.other), custom_call_target="tpu_custom_call" | custom-call | tf_op jit(solution)/shard_map/pack/pallas_call | solution.py:260
  8.5 3.8 %collective-permute-start.18 = (bf16[3,13,32,128]{3,2,1,0:T(8,128)(2,1)S(1)}, bf16[3,13,32,128]{3,2,1,0:T(8,128)(2,1)S(1)}, u32[]{:S(2)}, u32[]{:S(2)}) collective-permute-start(bf16[3,13,32,128]{3,2,1,0:T(8,128)(2,1)S(1)} %pack.1.refs_0_), channel_id=1, source_target_pairs={{0,112},{16,0},{32,16},{48,32},{64,48},{80,64},{96,80},{112,96},{1... | collective-permute-start | bytes 958472 | tf_op jit(solution)/shard_map/ppermute | solution.py:240
  12.2 1.2 %collective-permute-start.19 = (bf16[3,13,32,128]{3,2,1,0:T(8,128)(2,1)S(1)}, bf16[3,13,32,128]{3,2,1,0:T(8,128)(2,1)S(1)}, u32[]{:S(2)}, u32[]{:S(2)}) collective-permute-start(bf16[3,13,32,128]{3,2,1,0:T(8,128)(2,1)S(1)} %pack.1.refs_0_), channel_id=1, source_target_pairs={{0,128},{16,144},{32,160},{48,176},{64,192},{80,208},{96,224},{112... | collective-permute-start | bytes 958472 | tf_op jit(solution)/shard_map/ppermute | solution.py:241
  13.4 6.3 %collective-permute-done.17.refs_7_ = bf16[3,13,32,128]{3,2,1,0:T(8,128)(2,1)S(1)} collective-permute-done((bf16[3,13,32,128]{3,2,1,0:T(8,128)(2,1)S(1)}, bf16[3,13,32,128]{3,2,1,0:T(8,128)(2,1)S(1)}, u32[]{:S(2)}, u32[]{:S(2)}) %collective-permute-start.17) | collective-permute-done | bytes 319520 | tf_op jit(solution)/shard_map/ppermute | solution.py:239
  20.7 2.7 %collective-permute-start.21 = (bf16[3,13,32,128]{3,2,1,0:T(8,128)(2,1)S(1)}, bf16[3,13,32,128]{3,2,1,0:T(8,128)(2,1)S(1)}, u32[]{:S(2)}, u32[]{:S(2)}) collective-permute-start(bf16[3,13,32,128]{3,2,1,0:T(8,128)(2,1)S(1)} %collective-permute-done.18.refs_1_), channel_id=1, source_target_pairs={{0,112},{16,0},{32,16},{48,32},{64,48},{80,64},{96,80},{112,96},{1... | collective-permute-start | bytes 958472 | tf_op jit(solution)/shard_map/ppermute | solution.py:240
  23.4 1.2 %collective-permute-start.22 = (bf16[3,13,32,128]{3,2,1,0:T(8,128)(2,1)S(1)}, bf16[3,13,32,128]{3,2,1,0:T(8,128)(2,1)S(1)}, u32[]{:S(2)}, u32[]{:S(2)}) collective-permute-start(bf16[3,13,32,128]{3,2,1,0:T(8,128)(2,1)S(1)} %collective-permute-done.18.refs_1_), channel_id=1, source_target_pairs={{0,128},{16,144},{32,160},{48,176},{64,192},{80,208},{96,224},{112... | collective-permute-start | bytes 958472 | tf_op jit(solution)/shard_map/ppermute | solution.py:241
  24.9 4.6 %collective-permute-done.20.refs_6_ = bf16[3,13,32,128]{3,2,1,0:T(8,128)(2,1)S(1)} collective-permute-done((bf16[3,13,32,128]{3,2,1,0:T(8,128)(2,1)S(1)}, bf16[3,13,32,128]{3,2,1,0:T(8,128)(2,1)S(1)}, u32[]{:S(2)}, u32[]{:S(2)}) %collective-permute-start.20) | collective-permute-done | bytes 319520 | tf_op jit(solution)/shard_map/ppermute | solution.py:239
  30.4 2.7 %collective-permute-start.24 = (bf16[3,13,32,128]{3,2,1,0:T(8,128)(2,1)S(1)}, bf16[3,13,32,128]{3,2,1,0:T(8,128)(2,1)S(1)}, u32[]{:S(2)}, u32[]{:S(2)}) collective-permute-start(bf16[3,13,32,128]{3,2,1,0:T(8,128)(2,1)S(1)} %collective-permute-done.21.refs_2_), channel_id=1, source_target_pairs={{0,112},{16,0},{32,16},{48,32},{64,48},{80,64},{96,80},{112,96},{1... | collective-permute-start | bytes 958472 | tf_op jit(solution)/shard_map/ppermute | solution.py:240
  33.3 3.9 %collective-permute-done.25.refs_15_ = bf16[3,13,32,128]{3,2,1,0:T(8,128)(2,1)S(1)} collective-permute-done((bf16[3,13,32,128]{3,2,1,0:T(8,128)(2,1)S(1)}, bf16[3,13,32,128]{3,2,1,0:T(8,128)(2,1)S(1)}, u32[]{:S(2)}, u32[]{:S(2)}) %collective-permute-start.25) | collective-permute-done | bytes 319520 | tf_op jit(solution)/shard_map/ppermute | solution.py:241
  38.1 1.1 %collective-permute-start.28 = (bf16[3,13,32,128]{3,2,1,0:T(8,128)(2,1)S(1)}, bf16[3,13,32,128]{3,2,1,0:T(8,128)(2,1)S(1)}, u32[]{:S(2)}, u32[]{:S(2)}) collective-permute-start(bf16[3,13,32,128]{3,2,1,0:T(8,128)(2,1)S(1)} %collective-permute-done.24.refs_3_), channel_id=1, source_target_pairs={{0,128},{16,144},{32,160},{48,176},{64,192},{80,208},{96,224},{112... | collective-permute-start | bytes 958472 | tf_op jit(solution)/shard_map/ppermute | solution.py:241
  39.5 1.4 %collective-permute-done.27.refs_10_ = bf16[3,13,32,128]{3,2,1,0:T(8,128)(2,1)S(1)} collective-permute-done((bf16[3,13,32,128]{3,2,1,0:T(8,128)(2,1)S(1)}, bf16[3,13,32,128]{3,2,1,0:T(8,128)(2,1)S(1)}, u32[]{:S(2)}, u32[]{:S(2)}) %collective-permute-start.27) | collective-permute-done | bytes 319520 | tf_op jit(solution)/shard_map/ppermute | solution.py:240
  40.9 2.0 %collective-permute-start.29 = (bf16[3,13,32,128]{3,2,1,0:T(8,128)(2,1)S(1)}, bf16[3,13,32,128]{3,2,1,0:T(8,128)(2,1)S(1)}, u32[]{:S(2)}, u32[]{:S(2)}) collective-permute-start(bf16[3,13,32,128]{3,2,1,0:T(8,128)(2,1)S(1)} %collective-permute-done.25.refs_15_), channel_id=1, source_target_pairs={{0,16},{16,32},{32,48},{48,64},{64,80},{80,96},{96,112},{112,0},{1... | collective-permute-start | bytes 958472 | tf_op jit(solution)/shard_map/ppermute | solution.py:239
  42.9 3.9 %collective-permute-done.26.refs_4_ = bf16[3,13,32,128]{3,2,1,0:T(8,128)(2,1)S(1)} collective-permute-done((bf16[3,13,32,128]{3,2,1,0:T(8,128)(2,1)S(1)}, bf16[3,13,32,128]{3,2,1,0:T(8,128)(2,1)S(1)}, u32[]{:S(2)}, u32[]{:S(2)}) %collective-permute-start.26) | collective-permute-done | bytes 319520 | tf_op jit(solution)/shard_map/ppermute | solution.py:239
  46.8 3.4 %collective-permute-done.29.refs_14_ = bf16[3,13,32,128]{3,2,1,0:T(8,128)(2,1)S(1)} collective-permute-done((bf16[3,13,32,128]{3,2,1,0:T(8,128)(2,1)S(1)}, bf16[3,13,32,128]{3,2,1,0:T(8,128)(2,1)S(1)}, u32[]{:S(2)}, u32[]{:S(2)}) %collective-permute-start.29) | collective-permute-done | bytes 319520 | tf_op jit(solution)/shard_map/ppermute | solution.py:239
  50.2 2.7 %collective-permute-done.30.refs_12_ = bf16[3,13,32,128]{3,2,1,0:T(8,128)(2,1)S(1)} collective-permute-done((bf16[3,13,32,128]{3,2,1,0:T(8,128)(2,1)S(1)}, bf16[3,13,32,128]{3,2,1,0:T(8,128)(2,1)S(1)}, u32[]{:S(2)}, u32[]{:S(2)}) %collective-permute-start.30) | collective-permute-done | bytes 319520 | tf_op jit(solution)/shard_map/ppermute | solution.py:240
  53.0 9.1 %main.1 = (f32[32,32,256]{2,1,0:T(8,128)S(1)}, f32[32,32,256]{2,1,0:T(8,128)S(1)}) custom-call(s32[32]{0:T(128)} %lv.7, s32[6]{0:T(128)} %lo.7, bf16[64,50,8,128]{3,2,1,0:T(8,128)(2,1)} %bitcast.37, bf16[64,50,8,128]{3,2,1,0:T(8,128)(2,1)S(1)} %collective-permute-done.16.w_other, bf16[3,13,32,128]{3,2,1,0:T(8,128)(2,1)S(1)} %pack.1.refs_0_, ...), custom_call_target="tpu_custom_call" | custom-call | tf_op jit(solution)/shard_map/main/pallas_call | solution.py:272
  62.1 4.9 %collective-permute-start.32 = (f32[32,32,256]{2,1,0:T(8,128)S(1)}, f32[32,32,256]{2,1,0:T(8,128)S(1)}, u32[]{:S(2)}, u32[]{:S(2)}) collective-permute-start(f32[32,32,256]{2,1,0:T(8,128)S(1)} %get-tuple-element.78), channel_id=1, source_target_pairs={{0,2},{2,0},{4,6},{6,4},{8,10},{10,8},{12,14},{14,12},{1,3},{3,1},... | collective-permute-start | bytes 3145736 | tf_op jit(solution)/shard_map/ppermute | solution.py:257
  67.0 2.3 %collective-permute-done.32 = f32[32,32,256]{2,1,0:T(8,128)S(1)} collective-permute-done((f32[32,32,256]{2,1,0:T(8,128)S(1)}, f32[32,32,256]{2,1,0:T(8,128)S(1)}, u32[]{:S(2)}, u32[]{:S(2)}) %collective-permute-start.32) | collective-permute-done | bytes 1048608 | tf_op jit(solution)/shard_map/ppermute | solution.py:257
  69.3 1.2 %add.36 = f32[32,32,256]{2,1,0:T(8,128)} add(f32[32,32,256]{2,1,0:T(8,128)S(1)} %get-tuple-element.77, f32[32,32,256]{2,1,0:T(8,128)S(1)} %collective-permute-done.32) | non-fusion elementwise | flops 262144 | bytes 3145728 | tf_op jit(solution)/shard_map/add | solution.py:292
  70.5 10.0 %all-to-all-start.1 = ((f32[32,32,256]{2,1,0:T(8,128)}), f32[32,32,256]{2,1,0:T(8,128)S(1)}, u32[]{:S(2)}, u32[]{:S(2)}) async-start(f32[32,32,256]{2,1,0:T(8,128)} %add.36), calls=%async_computation.1 | async-start | bytes 2097152 | tf_op jit(solution)/shard_map/all_to_all | solution.py:292
  80.5 15.6 %all-to-all-done.1.parts = f32[32,32,256]{2,1,0:T(8,128)S(1)} async-done(((f32[32,32,256]{2,1,0:T(8,128)}), f32[32,32,256]{2,1,0:T(8,128)S(1)}, u32[]{:S(2)}, u32[]{:S(2)}) %all-to-all-start.1) | async-done | bytes 1048608 | tf_op jit(solution)/shard_map/all_to_all | solution.py:292
  97.1 2.0 %last.1 = f32[512,64]{1,0:T(8,128)} custom-call(s32[32]{0:T(128)S(1)} %copy-done.9, s32[6]{0:T(128)S(1)} %copy-done.8, s32[1]{0:T(128)} %tier.1, f32[32,32,256]{2,1,0:T(8,128)S(1)} %all-to-all-done.1.parts, f32[512,64]{1,0:T(8,128)S(1)} %get-tuple-element.93.other), custom_call_target="tpu_custom_call" | custom-call | tf_op jit(solution)/shard_map/last/pallas_call | solution.py:295
  (27 shorter events, 5.2 us)
Async XLA Ops:
  0.0 5.4 %collective-permute-start.15 = (bf16[50,64,128]{2,1,0:T(8,128)(2,1)}, bf16[50,64,128]{2,1,0:T(8,128)(2,1)S(1)}, u32[]{:S(2)}, u32[]{:S(2)}) collective-permute-start(bf16[50,64,128]{2,1,0:T(8,128)(2,1)} %own.1), channel_id=1, source_target_pairs={{0,2},{2,0},{4,6},{6,4},{8,10},{10,8},{12,14},{14,12},{1,3},{3,1},... | collective-permute-start | bytes 2457608 | tf_op jit(solution)/shard_map/ppermute | solution.py:257
  7.7 89.0 %copy-start.1 = (bf16[50,64,128]{2,1,0:T(8,128)(2,1)S(1)}, bf16[50,64,128]{2,1,0:T(8,128)(2,1)}, u32[]{:S(2)}) copy-start(bf16[50,64,128]{2,1,0:T(8,128)(2,1)} %own.1) | copy-start | bytes 2457604
  7.7 89.0 %copy-start.8 = (s32[6]{0:T(128)S(1)}, s32[6]{0:T(128)}, u32[]{:S(2)}) copy-start(s32[6]{0:T(128)} %lo.7) | copy-start | bytes 76
  7.7 89.0 %copy-start.9 = (s32[32]{0:T(128)S(1)}, s32[32]{0:T(128)}, u32[]{:S(2)}) copy-start(s32[32]{0:T(128)} %lv.7) | copy-start | bytes 388
  7.8 45.2 %collective-permute-start.16 = (bf16[64,50,8,128]{3,2,1,0:T(8,128)(2,1)}, bf16[64,50,8,128]{3,2,1,0:T(8,128)(2,1)S(1)}, u32[]{:S(2)}, u32[]{:S(2)}) collective-permute-start(bf16[64,50,8,128]{3,2,1,0:T(8,128)(2,1)} %bitcast.36), channel_id=1, source_target_pairs={{0,2},{2,0},{4,6},{6,4},{8,10},{10,8},{12,14},{14,12},{1,3},{3,1},... | collective-permute-start | bytes 19660808 | tf_op jit(solution)/shard_map/ppermute | solution.py:257
  8.5 11.3 %collective-permute-start.17 = (bf16[3,13,32,128]{3,2,1,0:T(8,128)(2,1)S(1)}, bf16[3,13,32,128]{3,2,1,0:T(8,128)(2,1)S(1)}, u32[]{:S(2)}, u32[]{:S(2)}) collective-permute-start(bf16[3,13,32,128]{3,2,1,0:T(8,128)(2,1)S(1)} %pack.1.refs_0_), channel_id=1, source_target_pairs={{0,16},{16,32},{32,48},{48,64},{64,80},{80,96},{96,112},{112,0},{1... | collective-permute-start | bytes 958472 | tf_op jit(solution)/shard_map/ppermute | solution.py:239
  8.5 11.3 %collective-permute-start.18 = (bf16[3,13,32,128]{3,2,1,0:T(8,128)(2,1)S(1)}, bf16[3,13,32,128]{3,2,1,0:T(8,128)(2,1)S(1)}, u32[]{:S(2)}, u32[]{:S(2)}) collective-permute-start(bf16[3,13,32,128]{3,2,1,0:T(8,128)(2,1)S(1)} %pack.1.refs_0_), channel_id=1, source_target_pairs={{0,112},{16,0},{32,16},{48,32},{64,48},{80,64},{96,80},{112,96},{1... | collective-permute-start | bytes 958472 | tf_op jit(solution)/shard_map/ppermute | solution.py:240
  12.2 8.5 %collective-permute-start.19 = (bf16[3,13,32,128]{3,2,1,0:T(8,128)(2,1)S(1)}, bf16[3,13,32,128]{3,2,1,0:T(8,128)(2,1)S(1)}, u32[]{:S(2)}, u32[]{:S(2)}) collective-permute-start(bf16[3,13,32,128]{3,2,1,0:T(8,128)(2,1)S(1)} %pack.1.refs_0_), channel_id=1, source_target_pairs={{0,128},{16,144},{32,160},{48,176},{64,192},{80,208},{96,224},{112... | collective-permute-start | bytes 958472 | tf_op jit(solution)/shard_map/ppermute | solution.py:241
  20.7 8.8 %collective-permute-start.20 = (bf16[3,13,32,128]{3,2,1,0:T(8,128)(2,1)S(1)}, bf16[3,13,32,128]{3,2,1,0:T(8,128)(2,1)S(1)}, u32[]{:S(2)}, u32[]{:S(2)}) collective-permute-start(bf16[3,13,32,128]{3,2,1,0:T(8,128)(2,1)S(1)} %collective-permute-done.17.refs_7_), channel_id=1, source_target_pairs={{0,16},{16,32},{32,48},{48,64},{64,80},{80,96},{96,112},{112,0},{1... | collective-permute-start | bytes 958472 | tf_op jit(solution)/shard_map/ppermute | solution.py:239
  20.7 8.8 %collective-permute-start.21 = (bf16[3,13,32,128]{3,2,1,0:T(8,128)(2,1)S(1)}, bf16[3,13,32,128]{3,2,1,0:T(8,128)(2,1)S(1)}, u32[]{:S(2)}, u32[]{:S(2)}) collective-permute-start(bf16[3,13,32,128]{3,2,1,0:T(8,128)(2,1)S(1)} %collective-permute-done.18.refs_1_), channel_id=1, source_target_pairs={{0,112},{16,0},{32,16},{48,32},{64,48},{80,64},{96,80},{112,96},{1... | collective-permute-start | bytes 958472 | tf_op jit(solution)/shard_map/ppermute | solution.py:240
  23.4 7.0 %collective-permute-start.22 = (bf16[3,13,32,128]{3,2,1,0:T(8,128)(2,1)S(1)}, bf16[3,13,32,128]{3,2,1,0:T(8,128)(2,1)S(1)}, u32[]{:S(2)}, u32[]{:S(2)}) collective-permute-start(bf16[3,13,32,128]{3,2,1,0:T(8,128)(2,1)S(1)} %collective-permute-done.18.refs_1_), channel_id=1, source_target_pairs={{0,128},{16,144},{32,160},{48,176},{64,192},{80,208},{96,224},{112... | collective-permute-start | bytes 958472 | tf_op jit(solution)/shard_map/ppermute | solution.py:241
  24.6 12.6 %collective-permute-start.25 = (bf16[3,13,32,128]{3,2,1,0:T(8,128)(2,1)S(1)}, bf16[3,13,32,128]{3,2,1,0:T(8,128)(2,1)S(1)}, u32[]{:S(2)}, u32[]{:S(2)}) collective-permute-start(bf16[3,13,32,128]{3,2,1,0:T(8,128)(2,1)S(1)} %collective-permute-done.17.refs_7_), channel_id=1, source_target_pairs={{0,128},{16,144},{32,160},{48,176},{64,192},{80,208},{96,224},{112... | collective-permute-start | bytes 958472 | tf_op jit(solution)/shard_map/ppermute | solution.py:241
  30.4 7.0 %collective-permute-start.23 = (bf16[3,13,32,128]{3,2,1,0:T(8,128)(2,1)S(1)}, bf16[3,13,32,128]{3,2,1,0:T(8,128)(2,1)S(1)}, u32[]{:S(2)}, u32[]{:S(2)}) collective-permute-start(bf16[3,13,32,128]{3,2,1,0:T(8,128)(2,1)S(1)} %collective-permute-done.20.refs_6_), channel_id=1, source_target_pairs={{0,16},{16,32},{32,48},{48,64},{64,80},{80,96},{96,112},{112,0},{1... | collective-permute-start | bytes 958472 | tf_op jit(solution)/shard_map/ppermute | solution.py:239
  30.4 7.0 %collective-permute-start.24 = (bf16[3,13,32,128]{3,2,1,0:T(8,128)(2,1)S(1)}, bf16[3,13,32,128]{3,2,1,0:T(8,128)(2,1)S(1)}, u32[]{:S(2)}, u32[]{:S(2)}) collective-permute-start(bf16[3,13,32,128]{3,2,1,0:T(8,128)(2,1)S(1)} %collective-permute-done.21.refs_2_), channel_id=1, source_target_pairs={{0,112},{16,0},{32,16},{48,32},{64,48},{80,64},{96,80},{112,96},{1... | collective-permute-start | bytes 958472 | tf_op jit(solution)/shard_map/ppermute | solution.py:240
  33.1 7.9 %collective-permute-start.27 = (bf16[3,13,32,128]{3,2,1,0:T(8,128)(2,1)S(1)}, bf16[3,13,32,128]{3,2,1,0:T(8,128)(2,1)S(1)}, u32[]{:S(2)}, u32[]{:S(2)}) collective-permute-start(bf16[3,13,32,128]{3,2,1,0:T(8,128)(2,1)S(1)} %collective-permute-done.22.refs_9_), channel_id=1, source_target_pairs={{0,112},{16,0},{32,16},{48,32},{64,48},{80,64},{96,80},{112,96},{1... | collective-permute-start | bytes 958472 | tf_op jit(solution)/shard_map/ppermute | solution.py:240
  37.4 9.4 %collective-permute-start.26 = (bf16[3,13,32,128]{3,2,1,0:T(8,128)(2,1)S(1)}, bf16[3,13,32,128]{3,2,1,0:T(8,128)(2,1)S(1)}, u32[]{:S(2)}, u32[]{:S(2)}) collective-permute-start(bf16[3,13,32,128]{3,2,1,0:T(8,128)(2,1)S(1)} %collective-permute-done.23.refs_5_), channel_id=1, source_target_pairs={{0,16},{16,32},{32,48},{48,64},{64,80},{80,96},{96,112},{112,0},{1... | collective-permute-start | bytes 958472 | tf_op jit(solution)/shard_map/ppermute | solution.py:239
  38.1 8.8 %collective-permute-start.28 = (bf16[3,13,32,128]{3,2,1,0:T(8,128)(2,1)S(1)}, bf16[3,13,32,128]{3,2,1,0:T(8,128)(2,1)S(1)}, u32[]{:S(2)}, u32[]{:S(2)}) collective-permute-start(bf16[3,13,32,128]{3,2,1,0:T(8,128)(2,1)S(1)} %collective-permute-done.24.refs_3_), channel_id=1, source_target_pairs={{0,128},{16,144},{32,160},{48,176},{64,192},{80,208},{96,224},{112... | collective-permute-start | bytes 958472 | tf_op jit(solution)/shard_map/ppermute | solution.py:241
  39.1 11.1 %collective-permute-start.31 = (bf16[3,13,32,128]{3,2,1,0:T(8,128)(2,1)S(1)}, bf16[3,13,32,128]{3,2,1,0:T(8,128)(2,1)S(1)}, u32[]{:S(2)}, u32[]{:S(2)}) collective-permute-start(bf16[3,13,32,128]{3,2,1,0:T(8,128)(2,1)S(1)} %collective-permute-done.23.refs_5_), channel_id=1, source_target_pairs={{0,128},{16,144},{32,160},{48,176},{64,192},{80,208},{96,224},{112... | collective-permute-start | bytes 958472 | tf_op jit(solution)/shard_map/ppermute | solution.py:241
  40.9 9.3 %collective-permute-start.29 = (bf16[3,13,32,128]{3,2,1,0:T(8,128)(2,1)S(1)}, bf16[3,13,32,128]{3,2,1,0:T(8,128)(2,1)S(1)}, u32[]{:S(2)}, u32[]{:S(2)}) collective-permute-start(bf16[3,13,32,128]{3,2,1,0:T(8,128)(2,1)S(1)} %collective-permute-done.25.refs_15_), channel_id=1, source_target_pairs={{0,16},{16,32},{32,48},{48,64},{64,80},{80,96},{96,112},{112,0},{1... | collective-permute-start | bytes 958472 | tf_op jit(solution)/shard_map/ppermute | solution.py:239
  46.8 6.1 %collective-permute-start.30 = (bf16[3,13,32,128]{3,2,1,0:T(8,128)(2,1)S(1)}, bf16[3,13,32,128]{3,2,1,0:T(8,128)(2,1)S(1)}, u32[]{:S(2)}, u32[]{:S(2)}) collective-permute-start(bf16[3,13,32,128]{3,2,1,0:T(8,128)(2,1)S(1)} %collective-permute-done.28.refs_11_), channel_id=1, source_target_pairs={{0,112},{16,0},{32,16},{48,32},{64,48},{80,64},{96,80},{112,96},{1... | collective-permute-start | bytes 958472 | tf_op jit(solution)/shard_map/ppermute | solution.py:240
  62.1 7.2 %collective-permute-start.32 = (f32[32,32,256]{2,1,0:T(8,128)S(1)}, f32[32,32,256]{2,1,0:T(8,128)S(1)}, u32[]{:S(2)}, u32[]{:S(2)}) collective-permute-start(f32[32,32,256]{2,1,0:T(8,128)S(1)} %get-tuple-element.78), channel_id=1, source_target_pairs={{0,2},{2,0},{4,6},{6,4},{8,10},{10,8},{12,14},{14,12},{1,3},{3,1},... | collective-permute-start | bytes 3145736 | tf_op jit(solution)/shard_map/ppermute | solution.py:257
  70.5 25.6 %all-to-all-start.1 = ((f32[32,32,256]{2,1,0:T(8,128)}), f32[32,32,256]{2,1,0:T(8,128)S(1)}, u32[]{:S(2)}, u32[]{:S(2)}) async-start(f32[32,32,256]{2,1,0:T(8,128)} %add.36), calls=%async_computation.1 | async-start | bytes 2097152 | tf_op jit(solution)/shard_map/all_to_all | solution.py:292

commit v3 on v2

--- a/solution.py
+++ b/solution.py
@@ -1,3 +1,5 @@
+import functools
+
 import jax
 import jax.numpy as jnp
 from jax import lax
@@ -10,7 +12,8 @@
 KB = 25
 HALF = 13
 GROUPS = 3
-SLOTS = 8
+EARLY = (0, 1, 2, 3, 4, 5, 6, 7, 8, 9, 10, 11, 15)
+LATE = (12, 13, 14)
 SMEM = pltpu.MemorySpace.SMEM
 VMEM = pltpu.MemorySpace.VMEM
 I32 = jnp.int32
@@ -45,6 +48,7 @@
     gx, gy, gz = lax.axis_index("gx"), lax.axis_index("gy"), lax.axis_index("gz")
     core = gy % 2
     lanes = lax.broadcasted_iota(I32, (HALF, 32, 128), 2)
+    rows = lax.broadcasted_iota(I32, (HALF, 32, 128), 0)
     out[...] = jnp.zeros_like(out)
     room = 2 * GROUPS
 
@@ -63,7 +67,8 @@
                     part = amp[pl.ds(kap * KB + 12 * half, HALF), pl.ds(pl.multiple_of(beta * 32, 32), 32), :]
                     to = spot + 32 * half
                     moved = pltpu.roll(part.astype(F32), jnp.bitwise_and(to - gam * 32 + 128, 127), 2)
-                    value = jnp.where((lanes >= to) & (lanes < to + 32), moved, value)
+                    take = (lanes >= to) & (lanes < to + 32) & (rows >= half)
+                    value = jnp.where(take, moved, value)
                 out[unit // 2] = value.astype(BF16)
 
             return seen + jnp.where(hit, 1, 0), unit + jnp.where(put, 1, 0)
@@ -74,17 +79,17 @@
     add(other, 1 - core, False)(unit)
 
 
-def main_kernel(lv, lo, w_own, w_other, *refs):
-    chunks = refs[:16]
-    keep, send = refs[16:18]
-    w, spare, t, acc, pairs, units, blocks, busy, w_sem, spare_sem = refs[18:]
+def main_kernel(arrived, slots, lv, lo, w_own, w_other, *refs):
+    chunks, refs = dict(zip(arrived, refs)), refs[len(arrived) :]
+    before, refs = refs[:-12], refs[-12:]
+    keep, send, w, spare, t, acc, pairs, units, blocks, busy, w_sem, spare_sem = refs
     gx, gy, gz = lax.axis_index("gx"), lax.axis_index("gy"), lax.axis_index("gz")
     core = gy % 2
     x, z = gx // 8, gx % 8
     load_w = pltpu.make_async_copy(w_own, w, w_sem)
     load_w.start()
-    keep[...] = jnp.zeros_like(keep)
-    send[...] = jnp.zeros_like(send)
+    for i, total in enumerate((keep, send)):
+        total[...] = before[i][...] if before else jnp.zeros_like(total)
     room = 2 * GROUPS
 
     shift = lo[4] ^ lo[5]
@@ -102,13 +107,15 @@
                     def _():
                         pairs[alpha * 16 + plane * 8 + spot] = kap * 4 + gam
                 units[plane, label] = spot + 1
-    lanes = lax.broadcasted_iota(I32, (HALF, 32, 128), 2)
-
-    def count_both(i, most):
-        return tuple(n + jnp.where(lv[i] == lv[2 * gx + a] ^ shift, 1, 0) for a, n in enumerate(most))
-
-    most = lax.fori_loop(0, 32, count_both, (jnp.zeros((), I32), jnp.zeros((), I32)))
-    windows = (jnp.maximum(most[0], most[1]) + SLOTS - 1) // SLOTS
+    lanes = lax.broadcasted_iota(I32, (1, 32, 128), 2)
+
+    wants = [lv[2 * gx + alpha] ^ shift for alpha in range(2)]
+    most = [jnp.zeros((), I32)] * 2
+    for p in arrived:
+        source = (x ^ (p // 8)) * 8 + ((z + p) % 8)
+        for beta in range(2):
+            most = [n + jnp.where(lv[2 * source + beta] == want, 1, 0) for n, want in zip(most, wants)]
+    windows = (jnp.maximum(most[0], most[1]) + slots - 1) // slots
 
     def half_of_a(index, _):
         alpha, window = index // windows, index % windows
@@ -116,15 +123,15 @@
         for block in range(4):
             busy[block] = 0
 
-        slot = -SLOTS * window
-        for p in range(16):
+        slot = -slots * window
+        for p in arrived:
             source = (x ^ (p // 8)) * 8 + ((z + p) % 8)
 
             def arrival(beta, slot, p=p, source=source):
                 block = 2 * source + beta
                 hit = lv[block] == want
 
-                @pl.when(hit & (slot >= 0) & (slot < SLOTS))
+                @pl.when(hit & (slot >= 0) & (slot < slots))
                 def _():
                     blocks[slot] = block
                     own_first = jnp.where(beta == 0, 0, units[0, lv[2 * source]])
@@ -143,16 +150,16 @@
 
                         @pl.when(busy[line] == 0)
                         def _():
-                            t[pl.ds(line * KB, KB)] = jnp.zeros((KB, 32 * SLOTS, 128), BF16)
+                            t[pl.ds(line * KB, KB)] = jnp.zeros((KB, 32 * slots, 128), BF16)
                             busy[line] = 1
 
                         spot = (unit % 2) * 64
-                        whole = chunks[p][unit // 2].astype(F32)
-                        inside = (lanes >= gam * 32) & (lanes < gam * 32 + 32)
+                        whole = chunks[p][unit // 2]
+                        inside = ((lanes >= gam * 32) & (lanes < gam * 32 + 32)).astype(F32).astype(BF16)
                         for half in range(2):
                             moved = pltpu.roll(whole, jnp.bitwise_and(gam * 32 - spot - 32 * half + 256, 127), 2)
                             at = (pl.ds(line * KB + 12 * half, HALF), pl.ds(pl.multiple_of(slot * 32, 32), 32), slice(None))
-                            t[at] = jnp.where(inside, moved, t[at].astype(F32)).astype(BF16)
+                            t[at] = t[at] + moved * inside
                         return 0
 
                     lax.fori_loop(0, total, place, 0)
@@ -209,13 +216,17 @@
 
             return 0
 
-        lax.fori_loop(0, jnp.minimum(slot, SLOTS), give, 0)
+        lax.fori_loop(0, jnp.minimum(slot, slots), give, 0)
         return 0
 
     lax.fori_loop(0, 2 * windows, half_of_a, 0)
 
-
-def last_kernel(lv, lo, tier, parts, other, out):
+    @pl.when(windows == 0)
+    def _():
+        load_w.wait()
+
+
+def last_kernel(lv, lo, tier, parts, other, out, sem):
     gx, gy, gz = lax.axis_index("gx"), lax.axis_index("gy"), lax.axis_index("gz")
     dest = gy * 2 + gz
     shift = lo[4] ^ lo[5]
@@ -229,10 +240,16 @@
                     total = total + parts[2 * (y * 4 + alpha * 2 + g) + beta]
             cols.append(jnp.where(lv[2 * dest + beta] == label, total, 0.0))
         rows = slice(alpha * 256, alpha * 256 + 256)
-        out[rows, :] = jnp.where(tier[0] == 0, jnp.concatenate(cols, axis=0).T, other[rows, :])
-
-
-def gather_ring(mine):
+        out[rows, :] = jnp.concatenate(cols, axis=0).T
+
+    @pl.when(tier[0] == 1)
+    def _():
+        load = pltpu.make_async_copy(other, out, sem)
+        load.start()
+        load.wait()
+
+
+def gather_ring(mine, *extra):
     up = [(i, (i // 8) * 8 + (i + 1) % 8) for i in range(16)]
     down = [(i, (i // 8) * 8 + (i + 7) % 8) for i in range(16)]
     cross = [(i, (i + 8) % 16) for i in range(16)]
@@ -242,10 +259,10 @@
     hold = lax.optimization_barrier
     p1, m1, o0 = hold((zp(mine), zm(mine), xx(mine)))
     p2, m2, o1 = hold((zp(p1), zm(m1), xx(m1)))
-    p3, m3, o7 = hold((zp(p2), zm(m2), xx(p1)))
+    p3, m3, o7, *extra = hold((zp(p2), zm(m2), xx(p1), *extra))
     p4, o2, o3 = hold((zp(p3), zm(o1), xx(m3)))
     o6, o4, o5 = hold((zp(o7), zm(o3), xx(p3)))
-    return [mine, m1, m2, m3, p4, p3, p2, p1, o0, o1, o2, o3, o4, o5, o6, o7]
+    return [mine, m1, m2, m3, p4, p3, p2, p1, o0, o1, o2, o3, o4, o5, o6, o7], *extra
 
 
 def sparse(tier, integrals, amplitude, virtual_irrep, occupied_irrep):
@@ -266,37 +283,41 @@
         name="pack",
     )(virtual_irrep, occupied_irrep, amplitude, amp_other)
     packed, w = lax.optimization_barrier((packed, w))
-    w_other = swap(w)
     args = integrals, amplitude, virtual_irrep, occupied_irrep
-    chunks = gather_ring(packed)
-    keep, send = pl.pallas_call(
-        main_kernel,
-        out_shape=[jax.ShapeDtypeStruct((32, 32, 256), F32)] * 2,
-        in_specs=[smem, smem, hbm, hbm] + [vmem] * 16,
-        out_specs=[vmem, vmem],
-        scratch_shapes=[
-            pltpu.VMEM((64, 50, 8, 128), BF16),
-            pltpu.VMEM((32, KB, 8, 128), BF16),
-            pltpu.VMEM((100, 32 * SLOTS, 128), BF16),
-            pltpu.VMEM((32 * SLOTS, 256), F32),
-            pltpu.SMEM((32,), I32),
-            pltpu.SMEM((2, 8), I32),
-            pltpu.SMEM((32,), I32),
-            pltpu.SMEM((4,), I32),
-            pltpu.SemaphoreType.DMA,
-            pltpu.SemaphoreType.DMA,
-        ],
-        compiler_params=params,
-        name="main",
-    )(virtual_irrep, occupied_irrep, w, w_other, *chunks)
+    chunks, w_other = gather_ring(packed, swap(w))
+    before = []
+    for arrived, slots in ((EARLY, 8), (LATE, 4)):
+        before = pl.pallas_call(
+            functools.partial(main_kernel, arrived, slots),
+            out_shape=[jax.ShapeDtypeStruct((32, 32, 256), F32)] * 2,
+            in_specs=[smem, smem, hbm, hbm] + [vmem] * (len(arrived) + len(before)),
+            out_specs=[vmem, vmem],
+            scratch_shapes=[
+                pltpu.VMEM((64, 50, 8, 128), BF16),
+                pltpu.VMEM((32, KB, 8, 128), BF16),
+                pltpu.VMEM((100, 32 * slots, 128), BF16),
+                pltpu.VMEM((32 * slots, 256), F32),
+                pltpu.SMEM((32,), I32),
+                pltpu.SMEM((2, 8), I32),
+                pltpu.SMEM((32,), I32),
+                pltpu.SMEM((4,), I32),
+                pltpu.SemaphoreType.DMA,
+                pltpu.SemaphoreType.DMA,
+            ],
+            compiler_params=params,
+            cost_estimate=pl.CostEstimate(flops=slots * 10**9, bytes_accessed=slots * 3 * 10**6, transcendentals=0),
+            name="main" if slots == 8 else "rest",
+        )(virtual_irrep, occupied_irrep, w, w_other, *[chunks[p] for p in arrived], *before)
+    keep, send = before
     parts = lax.all_to_all(keep + swap(send), ("gy", "gz"), 0, 0, tiled=True)
     parts, late = lax.optimization_barrier((parts, tier))
     other = lax.cond(late[0] == 1, lambda: dense(*args), lambda: jnp.zeros((512, 64), F32))
     out = pl.pallas_call(
         last_kernel,
         out_shape=jax.ShapeDtypeStruct((512, 64), F32),
-        in_specs=[smem, smem, smem, vmem, vmem],
+        in_specs=[smem, smem, smem, vmem, hbm],
         out_specs=vmem,
+        scratch_shapes=[pltpu.SemaphoreType.DMA],
         compiler_params=params,
         name="last",
     )(virtual_irrep, occupied_irrep, tier, parts, other)
@@ -316,7 +337,7 @@
     masked = jnp.where((left_key == 0)[:, None, :, :], integrals, jnp.zeros((), integrals.dtype))
     masked = masked.reshape(rows_a * width_i, rows_k, rows_c)
     right_key = k_labels[:, None] ^ c_labels[None, :] ^ irrep_right
-    around = gather_ring(amplitude)
+    around, = gather_ring(amplitude)
     x, z = lax.axis_index("gx") // 8, lax.axis_index("gx") % 8
     piece = jnp.stack([jnp.concatenate(around[:8], axis=1), jnp.concatenate(around[8:], axis=1)])
     piece = jnp.roll(piece.reshape(2, rows_k, 8, 64, rows_c), (x, z), (0, 2))

time: 98.8 us -> 97.2 us (0.984)
  the two profiles are of different devices: /device:TPU:1 before, /device:TPU:71 now
where the time goes in v3:
time: 97.2 us; the launch traced here: 98.1 us
  waiting for transfers between devices  44.5 us (46%)
  starting transfers between devices  35.9 us (37%)
  Pallas kernels  15.2 us (16%)
  other arithmetic  1.2 us (1%)
  between operations  0.98 us (1%)
    all_to_all x1, waiting for transfers between devices, sparse(): parts = lax.all_to_all(keep + swap(send), ('gy', 'gz'), 0, 0, tiled=True)  15.1 us
    all_to_all x1, starting transfers between devices, sparse(): parts = lax.all_to_all(keep + swap(send), ('gy', 'gz'), 0, 0, tiled=True)  13.6 us
    ppermute x5, waiting for transfers between devices, gather_ring(): zp = lambda v: lax.ppermute(v, 'gx', up)  13.5 us
    ppermute x3, starting transfers between devices, sparse(): swap = lambda v: lax.ppermute(v, 'gy', [(i, i ^ 1) for i in range(8)])  10.9 us
    pallas_call x2, Pallas kernels, sparse(): pl.pallas_call(functools.partial(main_kernel, arrived, slots), out_shape=...  9.13 us
    ppermute x5, starting transfers between devices, gather_ring(): zp = lambda v: lax.ppermute(v, 'gx', up)  7.76 us
    ppermute x5, waiting for transfers between devices, gather_ring(): xx = lambda v: lax.ppermute(v, 'gx', cross)  6.65 us
    ppermute x5, waiting for transfers between devices, gather_ring(): zm = lambda v: lax.ppermute(v, 'gx', down)  6.45 us
  transfers between devices with their start and end apart: 19, of which 12 were waited for; matrix products, arithmetic and copies ran while one was open for 0% of the time, Pallas kernels for 8%

profile of v3, /device:TPU:71, one launch (start us, length us, event | category | flops | bytes accessed | tf_op | source)
XLA Modules:
  0.0 98.1 jit_solution(2986511797690264380)
XLA Ops:
  0.7 1.6 %tier.1 = s32[1]{0:T(128)} custom-call(s32[32]{0:T(128)} %lv.9, s32[6]{0:T(128)} %lo.9), custom_call_target="tpu_custom_call" | custom-call | tf_op jit(solution)/shard_map/tier/pallas_call | solution.py:359
  2.8 2.4 %pack.1.refs_0_ = bf16[3,13,32,128]{3,2,1,0:T(8,128)(2,1)S(1)} custom-call(s32[32]{0:T(128)} %lv.9, s32[6]{0:T(128)} %lo.9, bf16[50,64,128]{2,1,0:T(8,128)(2,1)} %own.1, bf16[50,64,128]{2,1,0:T(8,128)(2,1)S(1)} %collective-permute-done.15.other), custom_call_target="tpu_custom_call" | custom-call | tf_op jit(solution)/shard_map/pack/pallas_call | solution.py:277
  6.0 1.3 %collective-permute-start.16 = (bf16[3,13,32,128]{3,2,1,0:T(8,128)(2,1)S(1)}, bf16[3,13,32,128]{3,2,1,0:T(8,128)(2,1)S(1)}, u32[]{:S(2)}, u32[]{:S(2)}) collective-permute-start(bf16[3,13,32,128]{3,2,1,0:T(8,128)(2,1)S(1)} %pack.1.refs_0_), channel_id=1, source_target_pairs={{0,16},{16,32},{32,48},{48,64},{64,80},{80,96},{96,112},{112,0},{1... | collective-permute-start | bytes 958472 | tf_op jit(solution)/shard_map/ppermute | solution.py:256
  8.0 7.2 %collective-permute-done.16.refs_7_ = bf16[3,13,32,128]{3,2,1,0:T(8,128)(2,1)S(1)} collective-permute-done((bf16[3,13,32,128]{3,2,1,0:T(8,128)(2,1)S(1)}, bf16[3,13,32,128]{3,2,1,0:T(8,128)(2,1)S(1)}, u32[]{:S(2)}, u32[]{:S(2)}) %collective-permute-start.16) | collective-permute-done | bytes 319520 | tf_op jit(solution)/shard_map/ppermute | solution.py:256
  15.1 2.7 %collective-permute-done.17.refs_1_ = bf16[3,13,32,128]{3,2,1,0:T(8,128)(2,1)S(1)} collective-permute-done((bf16[3,13,32,128]{3,2,1,0:T(8,128)(2,1)S(1)}, bf16[3,13,32,128]{3,2,1,0:T(8,128)(2,1)S(1)}, u32[]{:S(2)}, u32[]{:S(2)}) %collective-permute-start.17) | collective-permute-done | bytes 319520 | tf_op jit(solution)/shard_map/ppermute | solution.py:257
  17.8 2.4 %collective-permute-start.19 = (bf16[3,13,32,128]{3,2,1,0:T(8,128)(2,1)S(1)}, bf16[3,13,32,128]{3,2,1,0:T(8,128)(2,1)S(1)}, u32[]{:S(2)}, u32[]{:S(2)}) collective-permute-start(bf16[3,13,32,128]{3,2,1,0:T(8,128)(2,1)S(1)} %collective-permute-done.16.refs_7_), channel_id=1, source_target_pairs={{0,16},{16,32},{32,48},{48,64},{64,80},{80,96},{96,112},{112,0},{1... | collective-permute-start | bytes 958472 | tf_op jit(solution)/shard_map/ppermute | solution.py:256
  20.5 1.2 %collective-permute-start.24 = (bf16[3,13,32,128]{3,2,1,0:T(8,128)(2,1)S(1)}, bf16[3,13,32,128]{3,2,1,0:T(8,128)(2,1)S(1)}, u32[]{:S(2)}, u32[]{:S(2)}) collective-permute-start(bf16[3,13,32,128]{3,2,1,0:T(8,128)(2,1)S(1)} %collective-permute-done.16.refs_7_), channel_id=1, source_target_pairs={{0,128},{16,144},{32,160},{48,176},{64,192},{80,208},{96,224},{112... | collective-permute-start | bytes 958472 | tf_op jit(solution)/shard_map/ppermute | solution.py:258
  21.6 4.3 %collective-permute-done.19.refs_6_ = bf16[3,13,32,128]{3,2,1,0:T(8,128)(2,1)S(1)} collective-permute-done((bf16[3,13,32,128]{3,2,1,0:T(8,128)(2,1)S(1)}, bf16[3,13,32,128]{3,2,1,0:T(8,128)(2,1)S(1)}, u32[]{:S(2)}, u32[]{:S(2)}) %collective-permute-start.19) | collective-permute-done | bytes 319520 | tf_op jit(solution)/shard_map/ppermute | solution.py:256
  25.9 1.7 %collective-permute-done.20.refs_2_ = bf16[3,13,32,128]{3,2,1,0:T(8,128)(2,1)S(1)} collective-permute-done((bf16[3,13,32,128]{3,2,1,0:T(8,128)(2,1)S(1)}, bf16[3,13,32,128]{3,2,1,0:T(8,128)(2,1)S(1)}, u32[]{:S(2)}, u32[]{:S(2)}) %collective-permute-start.20) | collective-permute-done | bytes 319520 | tf_op jit(solution)/shard_map/ppermute | solution.py:257
  27.6 2.0 %collective-permute-start.22 = (bf16[3,13,32,128]{3,2,1,0:T(8,128)(2,1)S(1)}, bf16[3,13,32,128]{3,2,1,0:T(8,128)(2,1)S(1)}, u32[]{:S(2)}, u32[]{:S(2)}) collective-permute-start(bf16[3,13,32,128]{3,2,1,0:T(8,128)(2,1)S(1)} %collective-permute-done.19.refs_6_), channel_id=1, source_target_pairs={{0,16},{16,32},{32,48},{48,64},{64,80},{80,96},{96,112},{112,0},{1... | collective-permute-start | bytes 958472 | tf_op jit(solution)/shard_map/ppermute | solution.py:256
  29.7 4.8 %collective-permute-done.24.refs_12_ = bf16[3,13,32,128]{3,2,1,0:T(8,128)(2,1)S(1)} collective-permute-done((bf16[3,13,32,128]{3,2,1,0:T(8,128)(2,1)S(1)}, bf16[3,13,32,128]{3,2,1,0:T(8,128)(2,1)S(1)}, u32[]{:S(2)}, u32[]{:S(2)}) %collective-permute-start.24) | collective-permute-done | bytes 319520 | tf_op jit(solution)/shard_map/ppermute | solution.py:258
  34.5 1.3 %collective-permute-done.23.refs_3_ = bf16[3,13,32,128]{3,2,1,0:T(8,128)(2,1)S(1)} collective-permute-done((bf16[3,13,32,128]{3,2,1,0:T(8,128)(2,1)S(1)}, bf16[3,13,32,128]{3,2,1,0:T(8,128)(2,1)S(1)}, u32[]{:S(2)}, u32[]{:S(2)}) %collective-permute-start.23) | collective-permute-done | bytes 319520 | tf_op jit(solution)/shard_map/ppermute | solution.py:257
  35.8 2.1 %collective-permute-start.27 = (bf16[3,13,32,128]{3,2,1,0:T(8,128)(2,1)S(1)}, bf16[3,13,32,128]{3,2,1,0:T(8,128)(2,1)S(1)}, u32[]{:S(2)}, u32[]{:S(2)}) collective-permute-start(bf16[3,13,32,128]{3,2,1,0:T(8,128)(2,1)S(1)} %collective-permute-done.22.refs_5_), channel_id=1, source_target_pairs={{0,16},{16,32},{32,48},{48,64},{64,80},{80,96},{96,112},{112,0},{1... | collective-permute-start | bytes 958472 | tf_op jit(solution)/shard_map/ppermute | solution.py:256
  38.1 1.3 %collective-permute-start.31 = (bf16[3,13,32,128]{3,2,1,0:T(8,128)(2,1)S(1)}, bf16[3,13,32,128]{3,2,1,0:T(8,128)(2,1)S(1)}, u32[]{:S(2)}, u32[]{:S(2)}) collective-permute-start(bf16[3,13,32,128]{3,2,1,0:T(8,128)(2,1)S(1)} %collective-permute-done.22.refs_5_), channel_id=1, source_target_pairs={{0,128},{16,144},{32,160},{48,176},{64,192},{80,208},{96,224},{112... | collective-permute-start | bytes 958472 | tf_op jit(solution)/shard_map/ppermute | solution.py:258
  40.1 2.1 %collective-permute-done.27.refs_4_ = bf16[3,13,32,128]{3,2,1,0:T(8,128)(2,1)S(1)} collective-permute-done((bf16[3,13,32,128]{3,2,1,0:T(8,128)(2,1)S(1)}, bf16[3,13,32,128]{3,2,1,0:T(8,128)(2,1)S(1)}, u32[]{:S(2)}, u32[]{:S(2)}) %collective-permute-start.27) | collective-permute-done | bytes 319520 | tf_op jit(solution)/shard_map/ppermute | solution.py:256
  42.2 1.8 %collective-permute-done.29.refs_11_ = bf16[3,13,32,128]{3,2,1,0:T(8,128)(2,1)S(1)} collective-permute-done((bf16[3,13,32,128]{3,2,1,0:T(8,128)(2,1)S(1)}, bf16[3,13,32,128]{3,2,1,0:T(8,128)(2,1)S(1)}, u32[]{:S(2)}, u32[]{:S(2)}) %collective-permute-start.29) | collective-permute-done | bytes 319520 | tf_op jit(solution)/shard_map/ppermute | solution.py:258
  44.1 6.4 %main.1 = (f32[32,32,256]{2,1,0:T(8,128)S(1)}, f32[32,32,256]{2,1,0:T(8,128)S(1)}) custom-call(s32[32]{0:T(128)} %lv.9, s32[6]{0:T(128)} %lo.9, bf16[64,50,8,128]{3,2,1,0:T(8,128)(2,1)} %bitcast.37, bf16[64,50,8,128]{3,2,1,0:T(8,128)(2,1)S(1)} %collective-permute-done.25.w_other, bf16[3,13,32,128]{3,2,1,0:T(8,128)(2,1)S(1)} %pack.1.refs_0_, ...), custom_call_target="tpu_custom_call" | custom-call | flops 8000000000 | bytes 24000000 | tf_op jit(solution)/shard_map/main/pallas_call | solution.py:290
  50.6 2.7 %rest.1 = (f32[32,32,256]{2,1,0:T(8,128)S(1)}, f32[32,32,256]{2,1,0:T(8,128)S(1)}) custom-call(s32[32]{0:T(128)S(1)} %copy-done.9, s32[6]{0:T(128)S(1)} %copy-done.8, bf16[64,50,8,128]{3,2,1,0:T(8,128)(2,1)S(1)} %bitcast.40, bf16[64,50,8,128]{3,2,1,0:T(8,128)(2,1)S(1)} %collective-permute-done.25.w_other, ...), custom_call_target="tpu_custom_call" | custom-call | flops 4000000000 | bytes 12000000 | tf_op jit(solution)/shard_map/rest/pallas_call | solution.py:290
  53.3 9.5 %collective-permute-start.32 = (f32[32,32,256]{2,1,0:T(8,128)S(1)}, f32[32,32,256]{2,1,0:T(8,128)S(1)}, u32[]{:S(2)}, u32[]{:S(2)}) collective-permute-start(f32[32,32,256]{2,1,0:T(8,128)S(1)} %get-tuple-element.84), channel_id=1, source_target_pairs={{0,2},{2,0},{4,6},{6,4},{8,10},{10,8},{12,14},{14,12},{1,3},{3,1},... | collective-permute-start | bytes 3145736 | tf_op jit(solution)/shard_map/ppermute | solution.py:274
  62.8 2.3 %collective-permute-done.32 = f32[32,32,256]{2,1,0:T(8,128)S(1)} collective-permute-done((f32[32,32,256]{2,1,0:T(8,128)S(1)}, f32[32,32,256]{2,1,0:T(8,128)S(1)}, u32[]{:S(2)}, u32[]{:S(2)}) %collective-permute-start.32) | collective-permute-done | bytes 1048608 | tf_op jit(solution)/shard_map/ppermute | solution.py:274
  65.1 1.2 %add.36 = f32[32,32,256]{2,1,0:T(8,128)} add(f32[32,32,256]{2,1,0:T(8,128)S(1)} %get-tuple-element.83, f32[32,32,256]{2,1,0:T(8,128)S(1)} %collective-permute-done.32) | non-fusion elementwise | flops 262144 | bytes 3145728 | tf_op jit(solution)/shard_map/add | solution.py:312
  66.3 13.6 %all-to-all-start.1 = ((f32[32,32,256]{2,1,0:T(8,128)}), f32[32,32,256]{2,1,0:T(8,128)S(1)}, u32[]{:S(2)}, u32[]{:S(2)}) async-start(f32[32,32,256]{2,1,0:T(8,128)} %add.36), calls=%async_computation.1 | async-start | bytes 2097152 | tf_op jit(solution)/shard_map/all_to_all | solution.py:312
  79.9 15.1 %all-to-all-done.1.parts = f32[32,32,256]{2,1,0:T(8,128)S(1)} async-done(((f32[32,32,256]{2,1,0:T(8,128)}), f32[32,32,256]{2,1,0:T(8,128)S(1)}, u32[]{:S(2)}, u32[]{:S(2)}) %all-to-all-start.1) | async-done | bytes 1048608 | tf_op jit(solution)/shard_map/all_to_all | solution.py:312
  95.9 2.0 %last.1 = f32[512,64]{1,0:T(8,128)} custom-call(s32[32]{0:T(128)S(1)} %copy-done.9, s32[6]{0:T(128)S(1)} %copy-done.8, s32[1]{0:T(128)} %tier.1, f32[32,32,256]{2,1,0:T(8,128)S(1)} %all-to-all-done.1.parts, f32[512,64]{1,0:T(8,128)S(1)} %get-tuple-element.99.other), custom_call_target="tpu_custom_call" | custom-call | tf_op jit(solution)/shard_map/last/pallas_call | solution.py:315
  (33 shorter events, 4.1 us)
Async XLA Ops:
  0.0 2.8 %collective-permute-start.15 = (bf16[50,64,128]{2,1,0:T(8,128)(2,1)}, bf16[50,64,128]{2,1,0:T(8,128)(2,1)S(1)}, u32[]{:S(2)}, u32[]{:S(2)}) collective-permute-start(bf16[50,64,128]{2,1,0:T(8,128)(2,1)} %own.1), channel_id=1, source_target_pairs={{0,2},{2,0},{4,6},{6,4},{8,10},{10,8},{12,14},{14,12},{1,3},{3,1},... | collective-permute-start | bytes 2457608 | tf_op jit(solution)/shard_map/ppermute | solution.py:274
  5.3 45.2 %slice-start = ((s8[6553600]{0:T(1024)(128)(4,1)}), s8[4194304]{0:T(1024)(128)(4,1)S(1)}, s32[]{:S(2)}) async-start(s8[6553600]{0:T(1024)(128)(4,1)} %bitcast.38), calls=%async_computation.2 | async-start | bytes 8388608
  5.3 45.2 %slice-start.1 = ((s8[6553600]{0:T(1024)(128)(4,1)}), s8[2359296]{0:T(1024)(128)(4,1)S(1)}, s32[]{:S(2)}) async-start(s8[6553600]{0:T(1024)(128)(4,1)} %bitcast.38), calls=%async_computation.3 | async-start | bytes 4718592
  5.3 45.2 %copy-start.8 = (s32[6]{0:T(128)S(1)}, s32[6]{0:T(128)}, u32[]{:S(2)}) copy-start(s32[6]{0:T(128)} %lo.9) | copy-start | bytes 76
  5.3 45.2 %copy-start.9 = (s32[32]{0:T(128)S(1)}, s32[32]{0:T(128)}, u32[]{:S(2)}) copy-start(s32[32]{0:T(128)} %lv.9) | copy-start | bytes 388
  5.3 30.5 %collective-permute-start.25 = (bf16[64,50,8,128]{3,2,1,0:T(8,128)(2,1)}, bf16[64,50,8,128]{3,2,1,0:T(8,128)(2,1)S(1)}, u32[]{:S(2)}, u32[]{:S(2)}) collective-permute-start(bf16[64,50,8,128]{3,2,1,0:T(8,128)(2,1)} %bitcast.36), channel_id=1, source_target_pairs={{0,2},{2,0},{4,6},{6,4},{8,10},{10,8},{12,14},{14,12},{1,3},{3,1},... | collective-permute-start | bytes 19660808 | tf_op jit(solution)/shard_map/ppermute | solution.py:274
  6.0 9.1 %collective-permute-start.16 = (bf16[3,13,32,128]{3,2,1,0:T(8,128)(2,1)S(1)}, bf16[3,13,32,128]{3,2,1,0:T(8,128)(2,1)S(1)}, u32[]{:S(2)}, u32[]{:S(2)}) collective-permute-start(bf16[3,13,32,128]{3,2,1,0:T(8,128)(2,1)S(1)} %pack.1.refs_0_), channel_id=1, source_target_pairs={{0,16},{16,32},{32,48},{48,64},{64,80},{80,96},{96,112},{112,0},{1... | collective-permute-start | bytes 958472 | tf_op jit(solution)/shard_map/ppermute | solution.py:256
  7.3 10.5 %collective-permute-start.17 = (bf16[3,13,32,128]{3,2,1,0:T(8,128)(2,1)S(1)}, bf16[3,13,32,128]{3,2,1,0:T(8,128)(2,1)S(1)}, u32[]{:S(2)}, u32[]{:S(2)}) collective-permute-start(bf16[3,13,32,128]{3,2,1,0:T(8,128)(2,1)S(1)} %pack.1.refs_0_), channel_id=1, source_target_pairs={{0,112},{16,0},{32,16},{48,32},{64,48},{80,64},{96,80},{112,96},{1... | collective-permute-start | bytes 958472 | tf_op jit(solution)/shard_map/ppermute | solution.py:257
  7.5 10.3 %collective-permute-start.18 = (bf16[3,13,32,128]{3,2,1,0:T(8,128)(2,1)S(1)}, bf16[3,13,32,128]{3,2,1,0:T(8,128)(2,1)S(1)}, u32[]{:S(2)}, u32[]{:S(2)}) collective-permute-start(bf16[3,13,32,128]{3,2,1,0:T(8,128)(2,1)S(1)} %pack.1.refs_0_), channel_id=1, source_target_pairs={{0,128},{16,144},{32,160},{48,176},{64,192},{80,208},{96,224},{112... | collective-permute-start | bytes 958472 | tf_op jit(solution)/shard_map/ppermute | solution.py:258
  17.8 8.1 %collective-permute-start.19 = (bf16[3,13,32,128]{3,2,1,0:T(8,128)(2,1)S(1)}, bf16[3,13,32,128]{3,2,1,0:T(8,128)(2,1)S(1)}, u32[]{:S(2)}, u32[]{:S(2)}) collective-permute-start(bf16[3,13,32,128]{3,2,1,0:T(8,128)(2,1)S(1)} %collective-permute-done.16.refs_7_), channel_id=1, source_target_pairs={{0,16},{16,32},{32,48},{48,64},{64,80},{80,96},{96,112},{112,0},{1... | collective-permute-start | bytes 958472 | tf_op jit(solution)/shard_map/ppermute | solution.py:256
  20.2 7.5 %collective-permute-start.20 = (bf16[3,13,32,128]{3,2,1,0:T(8,128)(2,1)S(1)}, bf16[3,13,32,128]{3,2,1,0:T(8,128)(2,1)S(1)}, u32[]{:S(2)}, u32[]{:S(2)}) collective-permute-start(bf16[3,13,32,128]{3,2,1,0:T(8,128)(2,1)S(1)} %collective-permute-done.17.refs_1_), channel_id=1, source_target_pairs={{0,112},{16,0},{32,16},{48,32},{64,48},{80,64},{96,80},{112,96},{1... | collective-permute-start | bytes 958472 | tf_op jit(solution)/shard_map/ppermute | solution.py:257
  20.2 7.5 %collective-permute-start.21 = (bf16[3,13,32,128]{3,2,1,0:T(8,128)(2,1)S(1)}, bf16[3,13,32,128]{3,2,1,0:T(8,128)(2,1)S(1)}, u32[]{:S(2)}, u32[]{:S(2)}) collective-permute-start(bf16[3,13,32,128]{3,2,1,0:T(8,128)(2,1)S(1)} %collective-permute-done.17.refs_1_), channel_id=1, source_target_pairs={{0,128},{16,144},{32,160},{48,176},{64,192},{80,208},{96,224},{112... | collective-permute-start | bytes 958472 | tf_op jit(solution)/shard_map/ppermute | solution.py:258
  20.5 14.0 %collective-permute-start.24 = (bf16[3,13,32,128]{3,2,1,0:T(8,128)(2,1)S(1)}, bf16[3,13,32,128]{3,2,1,0:T(8,128)(2,1)S(1)}, u32[]{:S(2)}, u32[]{:S(2)}) collective-permute-start(bf16[3,13,32,128]{3,2,1,0:T(8,128)(2,1)S(1)} %collective-permute-done.16.refs_7_), channel_id=1, source_target_pairs={{0,128},{16,144},{32,160},{48,176},{64,192},{80,208},{96,224},{112... | collective-permute-start | bytes 958472 | tf_op jit(solution)/shard_map/ppermute | solution.py:258
  27.6 6.8 %collective-permute-start.22 = (bf16[3,13,32,128]{3,2,1,0:T(8,128)(2,1)S(1)}, bf16[3,13,32,128]{3,2,1,0:T(8,128)(2,1)S(1)}, u32[]{:S(2)}, u32[]{:S(2)}) collective-permute-start(bf16[3,13,32,128]{3,2,1,0:T(8,128)(2,1)S(1)} %collective-permute-done.19.refs_6_), channel_id=1, source_target_pairs={{0,16},{16,32},{32,48},{48,64},{64,80},{80,96},{96,112},{112,0},{1... | collective-permute-start | bytes 958472 | tf_op jit(solution)/shard_map/ppermute | solution.py:256
  29.7 6.1 %collective-permute-start.23 = (bf16[3,13,32,128]{3,2,1,0:T(8,128)(2,1)S(1)}, bf16[3,13,32,128]{3,2,1,0:T(8,128)(2,1)S(1)}, u32[]{:S(2)}, u32[]{:S(2)}) collective-permute-start(bf16[3,13,32,128]{3,2,1,0:T(8,128)(2,1)S(1)} %collective-permute-done.20.refs_2_), channel_id=1, source_target_pairs={{0,112},{16,0},{32,16},{48,32},{64,48},{80,64},{96,80},{112,96},{1... | collective-permute-start | bytes 958472 | tf_op jit(solution)/shard_map/ppermute | solution.py:257
  29.7 10.4 %collective-permute-start.28 = (bf16[3,13,32,128]{3,2,1,0:T(8,128)(2,1)S(1)}, bf16[3,13,32,128]{3,2,1,0:T(8,128)(2,1)S(1)}, u32[]{:S(2)}, u32[]{:S(2)}) collective-permute-start(bf16[3,13,32,128]{3,2,1,0:T(8,128)(2,1)S(1)} %collective-permute-done.21.refs_9_), channel_id=1, source_target_pairs={{0,112},{16,0},{32,16},{48,32},{64,48},{80,64},{96,80},{112,96},{1... | collective-permute-start | bytes 958472 | tf_op jit(solution)/shard_map/ppermute | solution.py:257
  35.8 6.4 %collective-permute-start.27 = (bf16[3,13,32,128]{3,2,1,0:T(8,128)(2,1)S(1)}, bf16[3,13,32,128]{3,2,1,0:T(8,128)(2,1)S(1)}, u32[]{:S(2)}, u32[]{:S(2)}) collective-permute-start(bf16[3,13,32,128]{3,2,1,0:T(8,128)(2,1)S(1)} %collective-permute-done.22.refs_5_), channel_id=1, source_target_pairs={{0,16},{16,32},{32,48},{48,64},{64,80},{80,96},{96,112},{112,0},{1... | collective-permute-start | bytes 958472 | tf_op jit(solution)/shard_map/ppermute | solution.py:256
  37.9 6.1 %collective-permute-start.29 = (bf16[3,13,32,128]{3,2,1,0:T(8,128)(2,1)S(1)}, bf16[3,13,32,128]{3,2,1,0:T(8,128)(2,1)S(1)}, u32[]{:S(2)}, u32[]{:S(2)}) collective-permute-start(bf16[3,13,32,128]{3,2,1,0:T(8,128)(2,1)S(1)} %collective-permute-done.23.refs_3_), channel_id=1, source_target_pairs={{0,128},{16,144},{32,160},{48,176},{64,192},{80,208},{96,224},{112... | collective-permute-start | bytes 958472 | tf_op jit(solution)/shard_map/ppermute | solution.py:258
  38.1 12.4 %collective-permute-start.31 = (bf16[3,13,32,128]{3,2,1,0:T(8,128)(2,1)S(1)}, bf16[3,13,32,128]{3,2,1,0:T(8,128)(2,1)S(1)}, u32[]{:S(2)}, u32[]{:S(2)}) collective-permute-start(bf16[3,13,32,128]{3,2,1,0:T(8,128)(2,1)S(1)} %collective-permute-done.22.refs_5_), channel_id=1, source_target_pairs={{0,128},{16,144},{32,160},{48,176},{64,192},{80,208},{96,224},{112... | collective-permute-start | bytes 958472 | tf_op jit(solution)/shard_map/ppermute | solution.py:258
  39.4 11.1 %collective-permute-start.26 = (bf16[3,13,32,128]{3,2,1,0:T(8,128)(2,1)S(1)}, bf16[3,13,32,128]{3,2,1,0:T(8,128)(2,1)S(1)}, u32[]{:S(2)}, u32[]{:S(2)}) collective-permute-start(bf16[3,13,32,128]{3,2,1,0:T(8,128)(2,1)S(1)} %collective-permute-done.24.refs_12_), channel_id=1, source_target_pairs={{0,16},{16,32},{32,48},{48,64},{64,80},{80,96},{96,112},{112,0},{1... | collective-permute-start | bytes 958472 | tf_op jit(solution)/shard_map/ppermute | solution.py:256
  44.1 6.5 %collective-permute-start.30 = (bf16[3,13,32,128]{3,2,1,0:T(8,128)(2,1)S(1)}, bf16[3,13,32,128]{3,2,1,0:T(8,128)(2,1)S(1)}, u32[]{:S(2)}, u32[]{:S(2)}) collective-permute-start(bf16[3,13,32,128]{3,2,1,0:T(8,128)(2,1)S(1)} %collective-permute-done.29.refs_11_), channel_id=1, source_target_pairs={{0,112},{16,0},{32,16},{48,32},{64,48},{80,64},{96,80},{112,96},{1... | collective-permute-start | bytes 958472 | tf_op jit(solution)/shard_map/ppermute | solution.py:257
  50.6 45.0 %copy-start.1 = (bf16[50,64,128]{2,1,0:T(8,128)(2,1)S(1)}, bf16[50,64,128]{2,1,0:T(8,128)(2,1)}, u32[]{:S(2)}) copy-start(bf16[50,64,128]{2,1,0:T(8,128)(2,1)} %own.1) | copy-start | bytes 2457604
  53.3 11.8 %collective-permute-start.32 = (f32[32,32,256]{2,1,0:T(8,128)S(1)}, f32[32,32,256]{2,1,0:T(8,128)S(1)}, u32[]{:S(2)}, u32[]{:S(2)}) collective-permute-start(f32[32,32,256]{2,1,0:T(8,128)S(1)} %get-tuple-element.84), channel_id=1, source_target_pairs={{0,2},{2,0},{4,6},{6,4},{8,10},{10,8},{12,14},{14,12},{1,3},{3,1},... | collective-permute-start | bytes 3145736 | tf_op jit(solution)/shard_map/ppermute | solution.py:274
  66.3 28.7 %all-to-all-start.1 = ((f32[32,32,256]{2,1,0:T(8,128)}), f32[32,32,256]{2,1,0:T(8,128)S(1)}, u32[]{:S(2)}, u32[]{:S(2)}) async-start(f32[32,32,256]{2,1,0:T(8,128)} %add.36), calls=%async_computation.1 | async-start | bytes 2097152 | tf_op jit(solution)/shard_map/all_to_all | solution.py:312
